TPU v7x, 32 devices: a whole 2x2x4 slice. The times are simulated.
32 devices in a mesh: fsdp: 16 (over z, y, core), tensor: 2 (over x).
Axes of the slice: x: 2, y: 2, z: 4, core: 2. Of those that a mesh axis runs over, the one named last changes fastest.
Arguments:
- reference_hidden_states: bfloat16 [2048, 8192], P('fsdp'), may hold values from -6 to 6
- policy_hidden_states: bfloat16 [2048, 8192], P('fsdp'), may hold values from -6 to 6
- readout_target_rows: bfloat16 [2048, 8192], P('fsdp'), may hold values from -6 to 6
- final_norm_gain: bfloat16 [8192], replicated, may hold values from 0.5 to 1.5
- query_projection_matrix: bfloat16 [8192, 4096], P('fsdp', 'tensor'), may hold values from -0.0625 to 0.0625
- key_projection_matrix: bfloat16 [8192, 1024], P('fsdp', 'tensor'), may hold values from -0.0625 to 0.0625
- value_projection_matrix: bfloat16 [8192, 1024], P('fsdp', 'tensor'), may hold values from -0.0625 to 0.0625
- output_projection_matrix: bfloat16 [4096, 8192], P('tensor', 'fsdp'), may hold values from -0.09375 to 0.09375
- query_adapter_inner: bfloat16 [8192, 64], replicated, may hold values from -0.0625 to 0.0625
- query_adapter_outer: bfloat16 [64, 4096], P(None, 'tensor'), may hold values from -0.75 to 0.75
- value_adapter_inner: bfloat16 [8192, 64], replicated, may hold values from -0.0625 to 0.0625
- value_adapter_outer: bfloat16 [64, 1024], P(None, 'tensor'), may hold values from -0.75 to 0.75
- prompt_length: int32 [16], P('fsdp'), may hold values from 16 to 64
- preference_pair_index: int32 [16], replicated, may hold values from 0 to 15, each once
Outputs:
- dpo_loss: float32 [], replicated
- query_a_grad: float32 [8192, 64], P('tensor')
- query_outer_gradient: float32 [64, 4096], P(None, 'tensor')
- value_a_grad: float32 [8192, 64], P('tensor')
- value_outer_gradient: float32 [64, 1024], P(None, 'tensor')
Inputs may be any that keep to these rules, and one draw needn't show every extreme that they name: Pair i compares sequence preference_pair_index[2i] (chosen) with preference_pair_index[2i + 1] (rejected); every sequence appears exactly once.
All inputs are finite; a program needn't handle non-finite values.
Results may differ from a plain program's by a relative error of at most 0.018.
Values may be sent and summed in bfloat16 or wider, within the bound.
No kernel may reach another device: no remote copies, remote signals or barrier semaphores. Data moves between devices by JAX's collectives and lax.ppermute only.
A program may use at most 256 MiB of HBM per device.

v0:
```python
import functools

import jax
import jax.numpy as jnp
from jax import lax
from jax.experimental import pallas as pl
from jax.experimental.pallas import tpu as pltpu
from jax.sharding import PartitionSpec as P

QUERY_HEADS = 32
KEY_VALUE_HEADS = 8
HEAD_SIZE = 128
L = 128
GROUP = QUERY_HEADS // KEY_VALUE_HEADS
QCOLS = GROUP * HEAD_SIZE

adapter_scale = 0.5
dpo_beta = 0.1
loss_scale = 256.0
rope_base = 500000.0
norm_eps = 1e-05

F32 = jnp.float32
BF16 = jnp.bfloat16
ORD = (0, 2, 1, 3)
MB = 1 << 20
SMALL = pl.CostEstimate(flops=1, bytes_accessed=1, transcendentals=0)


def rope_tables(length, head_dim):
    half_dim = head_dim // 2
    exponent = jnp.arange(half_dim, dtype=F32) * (2.0 / head_dim)
    inverse = jnp.power(F32(rope_base), -exponent)
    angles = jnp.arange(length, dtype=F32)[:, None] * inverse[None, :]
    cosine = jnp.concatenate([jnp.cos(angles), jnp.cos(angles)], 1)
    sine = jnp.concatenate([-jnp.sin(angles), jnp.sin(angles)], 1)
    return cosine, sine


def dot(a, b, dims=((1,), (0,))):
    return lax.dot_general(a, b, (dims, ((), ())), preferred_element_type=F32)


def params(limit_mb):
    return pltpu.CompilerParams(vmem_limit_bytes=limit_mb * MB)


def smem():
    return pl.BlockSpec(memory_space=pltpu.SMEM)


def full(a):
    return pl.BlockSpec(a.shape, lambda i: (0,) * len(a.shape))


def prep_body(parts, part, split, idx, ref, pol, tgt, gain, *outs):
    x0, x1, x2, x3, t0, t1, t2, t3, go = outs[-9:]
    groups = parts // split
    for d, (xo, to) in enumerate(((x0, t0), (x1, t1), (x2, t2), (x3, t3))):
        for j in range(parts):
            src = pl.ds(pl.multiple_of(idx[d * parts + j] * part, part), part)
            cols = slice(j * part, (j + 1) * part)
            if xo.shape[0] == 2:
                xo[0, :, cols] = ref[:, src]
                xo[1, :, cols] = pol[:, src]
            else:
                @pl.when(idx[4 * parts + 4 * groups] == 0)
                def _():
                    xo[0, :, cols] = ref[:, src]

                @pl.when(idx[4 * parts + 4 * groups] != 0)
                def _():
                    xo[0, :, cols] = pol[:, src]

        for j in range(groups):
            at = idx[4 * parts + d * groups + j] * part
            src = pl.ds(pl.multiple_of(at, part), part)
            to[:, j * part : (j + 1) * part] = tgt[:, src]
            if d == 0:
                go[:, j * part : (j + 1) * part] = gain[:, src]


def prep(idx, ref, pol, tgt, gain, parts, part, split, marks=()):
    tokens = ref.shape[0]
    xs = lambda n: jax.ShapeDtypeStruct((n, tokens, parts * part), BF16)
    far = 1 if split == 2 else 2
    width = parts // split * part
    shapes = [xs(2), xs(2), xs(far), xs(far)]
    shapes += [jax.ShapeDtypeStruct((tokens, width), BF16)] * 4
    shapes += [jax.ShapeDtypeStruct((1, width), F32)]
    return pl.pallas_call(
        functools.partial(prep_body, parts, part, split),
        in_specs=[smem()] + [pl.BlockSpec(memory_space=pltpu.VMEM)] * (4 + len(marks)),
        out_specs=[pl.BlockSpec(memory_space=pltpu.VMEM)] * 9,
        out_shape=shapes,
        compiler_params=params(32),
        cost_estimate=SMALL,
    )(idx, ref, pol, tgt, gain, *marks)


def tile_of(cols):
    for tile in (256, 128):
        if cols % tile == 0:
            return tile
    return cols


def mm_body(count, x_ref, *refs):
    ws, outs = refs[:count], refs[-2:]
    total = None
    at = 0
    for w in ws:
        depth = w.shape[0]
        term = dot(x_ref[:, at : at + depth], w[...])
        total = term if total is None else total + term
        at += depth
    rows = total.shape[0] // 2
    for i, out_ref in enumerate(outs):
        out_ref[...] = total[i * rows : (i + 1) * rows].astype(out_ref.dtype)


def mm(x, half, ws, out_dtype, marks=()):
    rows, depth = x.shape[0] // 2, x.shape[1]
    cols = ws[0].shape[1]
    tile = tile_of(cols)
    return pl.pallas_call(
        functools.partial(mm_body, len(ws)),
        grid=(cols // tile,),
        in_specs=[pl.BlockSpec((rows, depth), lambda i: (half, 0))]
        + [pl.BlockSpec((w.shape[0], tile), lambda i: (0, i)) for w in ws]
        + [full(a) for a in marks],
        out_specs=[pl.BlockSpec((rows // 2, tile), lambda i: (0, i))] * 2,
        out_shape=[jax.ShapeDtypeStruct((rows // 2, cols), out_dtype)] * 2,
        compiler_params=params(32),
        cost_estimate=SMALL,
    )(x, *ws, *marks)


def out_body(n, row_parts, counts, *refs):
    ws = refs[row_parts * n :][: sum(counts)]
    out_ref, total = refs[-2:]
    for j in range(n):
        x = jnp.concatenate([refs[p * n + j][...] for p in range(row_parts)], 0)
        depth = x.shape[1]
        at = 0
        for k, count in enumerate(counts):
            row = j * depth
            piece = at
            while row >= ws[piece].shape[0]:
                row -= ws[piece].shape[0]
                piece += 1
            at += count
            term = dot(x, ws[piece][row : row + depth])
            if j:
                term = term + total[k]
            if j == n - 1:
                out_ref[k] = term.astype(BF16)
            else:
                total[k] = term


def out_mm(parts, ws, marks=()):
    n = len(parts[0])
    rows = sum(part[0].shape[0] for part in parts)
    cols = ws[0][0].shape[1]
    flat = [piece for w in ws for piece in w]
    inputs = [a for part in parts for a in part] + flat + list(marks)
    out_shape = jax.ShapeDtypeStruct((len(ws), rows, cols), BF16)
    return pl.pallas_call(
        functools.partial(out_body, n, len(parts), tuple(len(w) for w in ws)),
        grid=(1,),
        in_specs=[full(a) for a in inputs],
        out_specs=full(out_shape),
        out_shape=out_shape,
        scratch_shapes=[pltpu.VMEM(out_shape.shape, F32)],
        compiler_params=params(32),
        cost_estimate=SMALL,
    )(*inputs)


def back_body(counts, part, has_acc, x_ref, *refs):
    total = None
    at = 0
    for j, count in enumerate(counts):
        w = refs[at][...]
        if count == 2:
            w = jnp.where(pl.program_id(0) < pl.num_programs(0) // 2, w, refs[at + 1][...])
        at += count
        term = dot(x_ref[:, j * part : (j + 1) * part], w, ((1,), (1,)))
        total = term if total is None else total + term
    refs = refs[at:]
    if has_acc:
        total = total + refs[0][...]
        keep, send = refs[1:]
        half = total.shape[0] // 2
        keep[...] = total[:half]
        send[...] = total[half:].astype(send.dtype)
    else:
        refs[0][...] = total


def back_mm(x, half, ws, acc):
    rows = x.shape[0] // (1 if half is None else 2)
    depth = x.shape[1]
    part = ws[0][0].shape[1]
    heads = sum(piece.shape[0] for piece in ws[0])
    tile = min(512, heads)
    steps = heads // tile
    has_acc = acc is not None
    row = half or 0
    in_specs = [pl.BlockSpec((rows, depth), lambda i: (row, 0))]
    for w in ws:
        if len(w) == 1:
            in_specs.append(pl.BlockSpec((tile, part), lambda i: (i, 0)))
        else:
            in_specs.append(pl.BlockSpec((tile, part), lambda i: (jnp.minimum(i, steps // 2 - 1), 0)))
            in_specs.append(pl.BlockSpec((tile, part), lambda i: (jnp.maximum(i - steps // 2, 0), 0)))
    args = [x] + [piece for w in ws for piece in w]
    if has_acc:
        in_specs.append(pl.BlockSpec((rows, tile), lambda i: (0, i)))
        args.append(acc)
        out_specs = [pl.BlockSpec((rows // 2, tile), lambda i: (0, i))] * 2
        out_shape = [
            jax.ShapeDtypeStruct((rows // 2, heads), F32),
            jax.ShapeDtypeStruct((rows // 2, heads), BF16),
        ]
    else:
        out_specs = pl.BlockSpec((rows, tile), lambda i: (0, i))
        out_shape = jax.ShapeDtypeStruct((rows, heads), F32)
    return pl.pallas_call(
        functools.partial(back_body, tuple(len(w) for w in ws), part, has_acc),
        grid=(steps,),
        in_specs=in_specs,
        out_specs=out_specs,
        out_shape=out_shape,
        compiler_params=params(32),
        cost_estimate=SMALL,
    )(*args)


def causal(rows):
    at = lax.broadcasted_iota(jnp.int32, (rows, L), 0) % L
    return at >= lax.broadcasted_iota(jnp.int32, (rows, L), 1)


def probabilities(q4, keys):
    scores = dot(q4, keys, ((1,), (1,))) * (HEAD_SIZE**-0.5)
    weights = jnp.where(causal(q4.shape[0]), jnp.exp(scores), 0.0)
    return weights / jnp.sum(weights, -1, keepdims=True)


def stack_heads(values):
    return jnp.concatenate(
        [values[:, h * HEAD_SIZE : (h + 1) * HEAD_SIZE] for h in range(GROUP)], 0
    )


def attend_body(adapted, keep, rs, r2, low, qo, vo, cos_ref, sin_ref, *refs):
    mixed, *saved = refs[-1 - adapted :]
    cosine = cos_ref[...]
    sine = sin_ref[...]
    pre = keep[...] + rs[...].astype(F32) + r2[...].astype(F32)
    rank = qo.shape[0]
    q_pre = pre[:, :QCOLS]
    k_pre = pre[:, QCOLS : QCOLS + HEAD_SIZE]
    v_pre = pre[:, QCOLS + HEAD_SIZE :]
    if adapted:
        q_pre = q_pre + adapter_scale * dot(low[:, :rank], qo[...])
        v_pre = v_pre + adapter_scale * dot(low[:, rank:], vo[...])
    cos4 = jnp.concatenate([cosine] * GROUP, 0)
    sin4 = jnp.concatenate([sine] * GROUP, 0)
    q4 = stack_heads(q_pre)
    q4 = (q4 * cos4 + pltpu.roll(q4, HEAD_SIZE // 2, 1) * sin4).astype(BF16)
    keys = (k_pre * cosine + pltpu.roll(k_pre, HEAD_SIZE // 2, 1) * sine).astype(BF16)
    values = v_pre.astype(BF16)
    rounded = probabilities(q4, keys).astype(BF16)
    out = dot(rounded, values).astype(BF16)
    for h in range(GROUP):
        cols = slice(h * HEAD_SIZE, (h + 1) * HEAD_SIZE)
        mixed[:, cols] = out[h * L : (h + 1) * L]
        if saved:
            saved[0][:, cols] = q4[h * L : (h + 1) * L]
    if saved:
        saved[0][:, QCOLS : QCOLS + HEAD_SIZE] = keys
        saved[0][:, QCOLS + HEAD_SIZE :] = values


def attend(adapted, keep, rs, r2, low, qo, vo, group, cosine, sine, marks=()):
    each = QCOLS + 2 * HEAD_SIZE
    rank = qo.shape[0]
    top = lambda a: pl.BlockSpec((L, a.shape[1]), lambda i: (0, 0))
    return pl.pallas_call(
        functools.partial(attend_body, adapted),
        grid=(1,),
        in_specs=[
            top(keep),
            top(rs),
            top(r2),
            top(low),
            pl.BlockSpec((rank, QCOLS), lambda i: (0, group)),
            pl.BlockSpec((rank, HEAD_SIZE), lambda i: (0, group)),
            top(cosine),
            top(sine),
        ]
        + [full(a) for a in marks],
        out_specs=[pl.BlockSpec((L, w), lambda i: (0, 0)) for w in (QCOLS, each)[: 1 + adapted]],
        out_shape=[jax.ShapeDtypeStruct((L, w), BF16) for w in (QCOLS, each)[: 1 + adapted]],
        compiler_params=params(32),
        cost_estimate=SMALL,
    )(keep, rs, r2, low, qo, vo, cosine, sine, *marks)


def outer_place(block, rank, kv):
    wide = (kv * (GROUP + 1) + 1) // 2
    return (block // wide) * rank, (block % wide) * HEAD_SIZE, wide


def attend_back_body(kv, splits, keep, rs, r2, low, qo, vo, cos_ref, sin_ref, *refs):
    saved = refs[:splits]
    outer, mid = refs[splits:]
    rank = qo.shape[0]
    each = QCOLS + 2 * HEAD_SIZE
    cos4 = jnp.concatenate([cos_ref[...]] * GROUP, 0)
    sin4 = jnp.concatenate([sin_ref[...]] * GROUP, 0)
    low_q = low[:, :rank]
    low_v = low[:, rank:]
    q_mid = jnp.zeros((L, rank), F32)
    v_mid = jnp.zeros((L, rank), F32)

    def put(block, value):
        row, col, _ = outer_place(block, rank, kv)
        outer[row : row + rank, col : col + HEAD_SIZE] = adapter_scale * value

    if (kv * (GROUP + 1)) % 2:
        put(kv * (GROUP + 1), jnp.zeros((rank, HEAD_SIZE), F32))
    for j in range(kv):
        cols = slice(j * QCOLS, (j + 1) * QCOLS)
        at = (j % (kv // splits)) * each
        kept = saved[j // (kv // splits)]
        grad = keep[:, cols] + rs[:, cols].astype(F32) + r2[:, cols].astype(F32)
        grad4 = stack_heads(grad.astype(BF16))
        q4 = stack_heads(kept[:, at : at + QCOLS])
        keys = kept[:, at + QCOLS : at + QCOLS + HEAD_SIZE]
        values = kept[:, at + QCOLS + HEAD_SIZE : at + each]
        prob = probabilities(q4, keys)
        grad_prob = dot(grad4, values, ((1,), (1,)))
        grad_values = dot(prob.astype(BF16), grad4, ((0,), (0,))).astype(BF16)
        inner = jnp.sum(grad_prob * prob, -1, keepdims=True)
        grad_scores = (prob * (grad_prob - inner) * (HEAD_SIZE**-0.5)).astype(BF16)
        grad_query = dot(grad_scores, keys)
        back4 = (grad_query * cos4 - pltpu.roll(grad_query, HEAD_SIZE // 2, 1) * sin4).astype(BF16)
        for h in range(GROUP):
            at = j * GROUP + h
            back = back4[h * L : (h + 1) * L]
            put(at, dot(low_q, back, ((0,), (0,))))
            q_mid += dot(back, qo[:, at * HEAD_SIZE : (at + 1) * HEAD_SIZE], ((1,), (1,)))
        put(kv * GROUP + j, dot(low_v, grad_values, ((0,), (0,))))
        v_mid += dot(grad_values, vo[:, j * HEAD_SIZE : (j + 1) * HEAD_SIZE], ((1,), (1,)))
    mid[:, :rank] = (adapter_scale * q_mid).astype(BF16)
    mid[:, rank:] = (adapter_scale * v_mid).astype(BF16)


def attend_back(keep, rs, r2, low, qo, vo, cosine, sine, saved):
    rank = qo.shape[0]
    kv = vo.shape[1] // HEAD_SIZE
    wide = outer_place(0, rank, kv)[2]
    inputs = (keep, rs, r2, low, qo, vo, cosine, sine, *saved)
    shapes = [
        jax.ShapeDtypeStruct((2 * rank, wide * HEAD_SIZE), F32),
        jax.ShapeDtypeStruct((L, 2 * rank), BF16),
    ]
    return pl.pallas_call(
        functools.partial(attend_back_body, kv, len(saved)),
        grid=(1,),
        in_specs=[full(a) for a in inputs],
        out_specs=[full(a) for a in shapes],
        out_shape=shapes,
        compiler_params=params(32),
        cost_estimate=SMALL,
    )(*inputs)


def adapter_body(n, rows_each, scal, states, outer, *refs):
    mids = refs[:n]
    away, stay = refs[n:]
    src = pl.ds(pl.multiple_of(scal[0] * rows_each, rows_each), rows_each)
    own = states[:, src]
    total = None
    for mid in mids:
        term = dot(mid[...], own, ((0,), (0,)))
        total = term if total is None else total + term
    half = total.shape[0] // 2
    for low in range(2):
        rows = slice(low * half, (low + 1) * half)

        @pl.when(scal[1] == low)
        def _():
            stay[:, :rows_each] = total[rows]
            stay[:, rows_each:] = outer[rows]

        @pl.when(scal[1] != low)
        def _():
            away[:, :rows_each] = total[rows].astype(BF16)
            away[:, rows_each:] = outer[rows].astype(BF16)


def adapter_products(scal, states, mids, outer, rows_each):
    half = outer.shape[0] // 2
    cols = rows_each + outer.shape[1]
    shapes = [jax.ShapeDtypeStruct((half, cols), BF16), jax.ShapeDtypeStruct((half, cols), F32)]
    return pl.pallas_call(
        functools.partial(adapter_body, len(mids), rows_each),
        grid=(1,),
        in_specs=[smem()] + [full(a) for a in (states, outer, *mids)],
        out_specs=[full(a) for a in shapes],
        out_shape=shapes,
        compiler_params=params(32),
        cost_estimate=SMALL,
    )(scal, states, outer, *mids)


def assemble_body(rows_each, bit, own, other, q_inner, q_outer, v_inner, v_outer):
    low = jnp.where(bit[0] == 0, own[...], other[...]).astype(F32)
    high = jnp.where(bit[0] == 0, other[...], own[...]).astype(F32)
    q_inner[...] = low[:, :rows_each]
    v_inner[...] = high[:, :rows_each]
    outer = jnp.concatenate([low[:, rows_each:], high[:, rows_each:]], 1)
    cols = q_outer.shape[1]
    q_outer[...] = outer[:, :cols]
    v_outer[...] = outer[:, cols : cols + v_outer.shape[1]]


def assemble(bit, own, other, rows_each, q_cols, v_cols):
    rank = own.shape[0]
    shapes = [jax.ShapeDtypeStruct((rank, c), F32) for c in (rows_each, q_cols, rows_each, v_cols)]
    return pl.pallas_call(
        functools.partial(assemble_body, rows_each),
        grid=(1,),
        in_specs=[smem(), full(own), full(other)],
        out_specs=[full(a) for a in shapes],
        out_shape=shapes,
        compiler_params=params(32),
        cost_estimate=SMALL,
    )(bit, own, other)


def stats_body(counts, part, split, scal, xt_ref, xt_pol, tgt, gain, *refs):
    refs = list(refs)
    sums = []
    hidden_out, stats = refs[-2:]
    for which in range(2):
        xt = (xt_ref, xt_pol)[which]
        count = sum(counts)
        keeps = [r[i] for r in refs[: counts[0]] for i in range(r.shape[0])]
        recvs = [r[i] for r in refs[counts[0] : count] for i in range(r.shape[0])]
        refs = refs[count:]
        squares = jnp.zeros((L, HEAD_SIZE), F32)
        products = jnp.zeros((L, HEAD_SIZE), F32)
        for j, (keep, recv) in enumerate(zip(keeps, recvs)):
            src = pl.ds(pl.multiple_of((j * split + scal[0]) * part, part), part)
            hidden = xt[:, src].astype(F32) + keep.astype(F32) + recv.astype(F32)
            cols = slice(j * part, (j + 1) * part)
            if which == 1:
                hidden_out[0, :, cols] = hidden
            product = hidden * (gain[:, cols] * tgt[0, :, cols].astype(F32))
            square = hidden * hidden
            for s in range(part // HEAD_SIZE):
                lanes = slice(s * HEAD_SIZE, (s + 1) * HEAD_SIZE)
                squares += square[:, lanes]
                products += product[:, lanes]
        sums.append(
            [
                jnp.broadcast_to(jnp.sum(v, 1, keepdims=True), v.shape).T[:1]
                for v in (squares, products)
            ]
        )
    at = lax.broadcasted_iota(jnp.int32, (1, 2 * L), 1) % L
    own = (at >= scal[1]) & (pl.program_id(0) == 0)
    live = jnp.where(own, 1.0, 0.0).astype(F32)
    both = [jnp.concatenate([sums[0][i], sums[1][i]], 1) for i in range(2)]
    stats[...] = jnp.concatenate([*both, live, jnp.zeros((5, 2 * L), F32)], 0)


def norm_stats(scal, xt, tgt, gain, keeps, recvs, split):
    n = sum(a.shape[0] for a in keeps)
    part = keeps[0].shape[2]
    shared = []
    for which in range(2):
        at = functools.partial(lambda which, i: (0, 2 * i + which, 0), which)
        for a in (*keeps, *recvs):
            shared.append((a, pl.BlockSpec((a.shape[0], L, part), at)))
    return pl.pallas_call(
        functools.partial(stats_body, (len(keeps), len(recvs)), part, split),
        grid=(4,),
        in_specs=[
            smem(),
            pl.BlockSpec((L, xt.shape[1]), lambda i: ((i // 2) * 4 + i % 2, 0)),
            pl.BlockSpec((L, xt.shape[1]), lambda i: ((i // 2) * 4 + 2 + i % 2, 0)),
            pl.BlockSpec((1, L, n * part), lambda i: (i, 0, 0)),
            pl.BlockSpec((1, n * part), lambda i: (0, 0)),
        ]
        + [spec for _, spec in shared],
        out_specs=[
            pl.BlockSpec((1, L, n * part), lambda i: (i, 0, 0)),
            pl.BlockSpec((8, 2 * L), lambda i: (i, 0)),
        ],
        out_shape=[
            jax.ShapeDtypeStruct((4, L, n * part), F32),
            jax.ShapeDtypeStruct((32, 2 * L), F32),
        ],
        compiler_params=params(32),
        cost_estimate=SMALL,
    )(scal, xt, xt, tgt, gain, *[a for a, _ in shared])


def score_body(width, masks, ids, own, *refs):
    recvs = refs[: len(masks)]
    total_out, margin_out = refs[len(masks) :]
    lane = lax.broadcasted_iota(jnp.int32, (8, 128), 1)
    margins = jnp.zeros((8, 128), F32)
    for p in range(4):
        total = own[8 * p : 8 * p + 8]
        for recv, m in zip(recvs, masks):
            q = ORD.index(ORD[p] ^ m)
            total = total + recv[8 * q : 8 * q + 8]
        total_out[8 * p : 8 * p + 8] = total
        inverse = lax.rsqrt(total[0:1] * (1.0 / width) + norm_eps)
        score = total[1:2] * inverse * (width**-0.5)
        score = jnp.where(total[2:3] > 0.5, score, 0.0)
        margin = jnp.sum(score[:, L:], 1, keepdims=True) - jnp.sum(score[:, :L], 1, keepdims=True)
        margins = margins + jnp.where(lane == ids[p], margin, 0.0)
    margin_out[...] = margins


def scores(ids, own, recvs, masks, width):
    shapes = [jax.ShapeDtypeStruct(own.shape, F32), jax.ShapeDtypeStruct((8, 128), F32)]
    return pl.pallas_call(
        functools.partial(score_body, width, masks),
        grid=(1,),
        in_specs=[smem()] + [full(a) for a in (own, *recvs)],
        out_specs=[full(a) for a in shapes],
        out_shape=shapes,
        cost_estimate=SMALL,
    )(ids, own, *recvs)


def turn(i):
    return (2 * i + 1) % 5


def grad_body(width, seqs, n_vec, ids, pairs, total, hidden, tgt, gain, *refs):
    vecs = refs[:n_vec]
    grad_out, loss_out, slope = refs[n_vec:]
    lane = lax.broadcasted_iota(jnp.int32, (8, 128), 1)

    @pl.when(pl.program_id(0) == 0)
    def _():
        margin = vecs[0][...]
        for v in vecs[1:]:
            margin = margin + v[...]
        logits = jnp.zeros((8, 128), F32)
        for i in range(seqs // 2):
            sign = jnp.where(lane == pairs[2 * i], 1.0, 0.0) - jnp.where(
                lane == pairs[2 * i + 1], 1.0, 0.0
            )
            logit = dpo_beta * jnp.sum(margin * sign, 1, keepdims=True)
            logits = logits + jnp.where(lane == i, logit, 0.0)
        soft = jnp.maximum(-logits, 0.0) + jnp.log1p(jnp.exp(-jnp.abs(logits)))
        used = lane < seqs // 2
        loss = jnp.sum(jnp.where(used, soft, 0.0), 1, keepdims=True)
        loss_out[...] = jnp.broadcast_to(loss, (8, 128))
        slopes = jnp.where(used, -dpo_beta / (1.0 + jnp.exp(logits)), 0.0)
        gradient = jnp.zeros((8, 128), F32)
        for i in range(seqs // 2):
            each = jnp.sum(jnp.where(lane == i, slopes, 0.0), 1, keepdims=True)
            sign = jnp.where(lane == pairs[2 * i], 1.0, 0.0) - jnp.where(
                lane == pairs[2 * i + 1], 1.0, 0.0
            )
            gradient = gradient + each * sign
        slope[...] = gradient * loss_scale

    mine = lane == ids[turn(pl.program_id(0))]
    seq = jnp.sum(jnp.where(mine, slope[...], 0.0), 1, keepdims=True)[:1]
    rows = total[:, L:]
    token = jnp.where(rows[2:3] > 0.5, seq, 0.0) * (width**-0.5)
    inverse = lax.rsqrt(rows[0:1] * (1.0 / width) + norm_eps)
    first = inverse * token
    second = inverse * inverse * inverse * (token * rows[1:2] * (1.0 / width))
    first = jnp.broadcast_to(first, (L, L)).T
    second = jnp.broadcast_to(second, (L, L)).T
    for s in range(hidden.shape[2] // HEAD_SIZE):
        cols = slice(s * HEAD_SIZE, (s + 1) * HEAD_SIZE)
        weighted = gain[:, cols] * tgt[0, :, cols].astype(F32)
        grad_out[0, :, cols] = (first * weighted - second * hidden[0, :, cols]).astype(BF16)


def grad_hidden(ids, pairs, total, hidden, tgt, gain, vecs, width):
    n = hidden.shape[2]
    seqs = pairs.shape[0]
    return pl.pallas_call(
        functools.partial(grad_body, width, seqs, len(vecs)),
        grid=(4,),
        in_specs=[
            smem(),
            smem(),
            pl.BlockSpec((8, 2 * L), lambda i: (turn(i), 0)),
            pl.BlockSpec((1, L, n), lambda i: (turn(i), 0, 0)),
            pl.BlockSpec((1, L, n), lambda i: (turn(i), 0, 0)),
            pl.BlockSpec((1, n), lambda i: (0, 0)),
        ]
        + [pl.BlockSpec((8, 128), lambda i: (0, 0)) for _ in vecs],
        out_specs=[
            pl.BlockSpec((1, L, n), lambda i: (i, 0, 0)),
            pl.BlockSpec((8, 128), lambda i: (0, 0)),
        ],
        out_shape=[
            jax.ShapeDtypeStruct((4, L, n), BF16),
            jax.ShapeDtypeStruct((8, 128), F32),
        ],
        scratch_shapes=[pltpu.VMEM((8, 128), F32)],
        compiler_params=params(32),
        cost_estimate=SMALL,
    )(ids, pairs, total, hidden, tgt, gain, *vecs)


def per_device(
    fsdp_size,
    tensor_size,
    ref_states,
    pol_states,
    target_rows,
    norm_gain,
    wq,
    wk,
    wv,
    wo,
    qa,
    qo,
    va,
    vo,
    prompt_length,
    pairs,
):
    tokens, width = ref_states.shape
    groups = fsdp_size // 4
    near_z = fsdp_size // 4
    bits = []
    bit = 2
    while bit < fsdp_size:
        if bit != near_z:
            bits.append(bit)
        bit *= 2
    split = 2 if tensor_size == 2 and fsdp_size == 16 else 1
    kv_local = wk.shape[1] // HEAD_SIZE
    depth = wq.shape[0]
    part = depth // split
    rank = qa.shape[1]
    me = lax.axis_index("fsdp")
    x = lax.axis_index("tensor")
    side = x if split == 2 else 0

    def tmask(d):
        return (d & 1) | ((d >> 1) * near_z)

    def gmask(k):
        return sum(bit for i, bit in enumerate(bits) if (k >> i) & 1)

    def move(value, mask):
        return lax.ppermute(value, "fsdp", [(i, i ^ mask) for i in range(fsdp_size)])

    def swap_x(value):
        return lax.ppermute(value, "tensor", [(0, 1), (1, 0)])

    def move_both(value, mask, flip):
        pairs_list = [
            (2 * i + j, 2 * (i ^ mask) + (j ^ flip)) for i in range(fsdp_size) for j in range(2)
        ]
        return lax.ppermute(value, ("fsdp", "tensor"), pairs_list)

    def after(value, *others):
        return lax.optimization_barrier((value, *others))[0]

    def marker(*queue):
        return move(after(cosine[:16].astype(BF16), *queue), 1)

    cosine, sine = rope_tables(L, HEAD_SIZE)

    wide = groups == 4 and split == 2
    heads = wo.shape[0]

    def shard_of(j, *queue):
        q, k, v = wq, wk, wv
        if queue:
            q, k, v = lax.optimization_barrier((wq, wk, wv, *queue))[:3]
        pieces = [
            q[:, j * QCOLS : (j + 1) * QCOLS],
            k[:, j * HEAD_SIZE : (j + 1) * HEAD_SIZE],
            v[:, j * HEAD_SIZE : (j + 1) * HEAD_SIZE],
        ]
        return jnp.concatenate(pieces, 1)

    def gather(shard):
        return [shard] + [move(shard, gmask(k)) for k in range(1, groups)]

    if wide:
        over_y, over_z = gmask(1), gmask(2)
        shards = [shard_of(0)]
        zs = [move(shards[0], over_z)]
        ys = [move(shards[0], over_y)]
        corners = []

    parts = groups * split
    idx = []
    for d in range(4):
        for k in range(groups):
            for h in range(split):
                idx.append((me ^ tmask(d) ^ gmask(k)) * split + h)
    for d in range(4):
        for k in range(groups):
            idx.append((me ^ tmask(d) ^ gmask(k)) * split + side)
    idx.append(x)
    idx = jnp.stack(idx).astype(jnp.int32)
    marks = ()
    prepared = prep(
        idx,
        ref_states,
        pol_states,
        target_rows,
        norm_gain.astype(F32).reshape(1, width),
        parts,
        part,
        split,
        marks,
    )
    xs, ts, gain = prepared[:4], prepared[4:8], prepared[8]
    near = move(xs[1], 1)
    far = [move(xs[2], near_z)]
    far.append(move(xs[3], near_z | 1))

    if split == 2:
        other = [swap_x(a) for a in far]
        far = [
            [jnp.where(x == which, a[0], b[0]) for which in range(2)] for a, b in zip(far, other)
        ]
    states = jnp.concatenate(
        [
            *(xs[0][0], far[0][0], xs[0][1], far[0][1]),
            *(near[0], far[1][0], near[1], far[1][1]),
        ],
        0,
    )

    low = dot(pol_states, jnp.concatenate([qa, va], 1)).astype(BF16)
    cosine, sine = rope_tables(L, HEAD_SIZE)

    def own_columns(at, piece, *queue):
        return lax.dynamic_slice(
            after(wo, *queue), (piece * (heads // 2), at * part), (heads // 2, part)
        )

    def own_piece(step, *queue):
        at = (1 - x) if step < 2 else x
        return lax.dynamic_slice(
            after(wo, *queue), ((step % 2) * (heads // 2), at * part), (heads // 2, part)
        )

    def make_shard(j, *queue):
        if j < kv_local:
            shards.append(shard_of(j, *queue))
        elif j < kv_local + 4:
            shards.append(own_piece(j - kv_local, *queue))

    def next_shard(j, *more):
        queue = (zs[j - 1], ys[j - 1], *more)
        ys.append(move(after(shards[j], *queue), over_y))
        zs.append(move(after(shards[j], *queue), over_z))
        corners.append(move(after(*queue), over_y))

    saved = []
    parts_mixed = [[], [], []]

    def mix(j, keeps, came, sums, *queue, marks=()):
        results = []
        for which in range(2):
            total = sums[which * L : (which + 1) * L]
            result = attend(
                *(which == 1, keeps[which], came[which], total, low, qo, vo, j, cosine, sine),
                marks=marks,
            )
            saved.extend(result[1:])
            results.append(result[0])
        result = jnp.concatenate(results, 0)
        return result, move(after(result, *queue) if queue else result, near_z)

    def spread(result, other):
        far = move(jnp.concatenate([result, other], 0), 1)
        for part_mixed, value in zip(parts_mixed, (result, other, far)):
            part_mixed.append(value)
        return far

    if wide:
        make_shard(1, shards[0])
        next_shard(1)
        make_shard(2, zs[0])
    before = None
    ends = []
    for j in range(kv_local):
        if wide:
            marks = (marker(zs[j + 1], ys[j + 1]),)
            ws = [shards[j], ys[j], zs[j], corners[j]]
        else:
            ws = gather(shard_of(j))
        sends = mm(states, 1, ws, BF16, marks)
        came = [move(send, 1) for send in sends]
        keeps = mm(states, 0, ws, F32)
        if wide:
            next_shard(j + 2)
            make_shard(j + 3, zs[j + 1])
        over = jnp.concatenate(
            [(keeps[which][L:] + came[which][L:].astype(F32)).astype(BF16) for which in range(2)], 0
        )
        if before is not None:
            result, other = mix(j - 1, *before, *came, *ends)
            if j + 1 < kv_local:
                over = after(over, other)
            states = after(states, other)
            ends = [spread(result, other)]
        if wide:
            over = after(over, shards[-1])
        sums = move(over, near_z)
        if wide and j + 1 == kv_local:
            marks = (marker(zs[j + 2], ys[j + 2]),)
            make_shard(kv_local + 3, zs[-2])
        before = (keeps, came, sums)
    last = spread(*mix(kv_local - 1, *before, *ends, marks=marks))

    keeps, recvs = [], []
    if wide:
        next_shard(kv_local + 2, over)
        first = [a[kv_local : kv_local + 2] for a in (shards, ys, zs, corners)]
        marks = (marker(zs[-1], ys[-1]),)
        recvs.append(swap_x(out_mm(parts_mixed, first[:2], marks)))
        next_shard(kv_local + 3)
        recvs.append(swap_x(out_mm(parts_mixed, first[2:])))
        corners.append(move(after(zs[-1], ys[-1]), over_y))
        wo_send, wo_keep = first, [a[kv_local + 2 :] for a in (shards, ys, zs, corners)]
        keeps.append(out_mm(parts_mixed, wo_keep[:3]))
        keeps.append(out_mm(parts_mixed, wo_keep[3:]))
    else:
        wo_keep = [[w] for w in gather(wo)]
        product = out_mm(parts_mixed, wo_keep)
        if tensor_size > 1:
            product = lax.psum(product, "tensor")
        keeps.append(product)
        recvs.append(jnp.zeros_like(product))

    targets = [ts[0]] + [move(after(ts[d], last), tmask(d)) for d in (1, 2, 3)]
    tgt = jnp.stack([targets[d] for d in ORD])
    scal = jnp.stack([jnp.asarray(side, jnp.int32), prompt_length[0].astype(jnp.int32)])
    hidden, stats = norm_stats(scal, states, tgt, gain, keeps, recvs, split)
    masks, got = [], []
    for flip in range(split):
        for d in range(4):
            if d or flip:
                masks.append(d)
                if split == 2:
                    got.append(move_both(stats, tmask(d), flip))
                else:
                    got.append(move(stats, tmask(d)))
    ids = jnp.stack([me ^ tmask(d) for d in ORD]).astype(jnp.int32)
    total, margin = scores(ids, stats, got, tuple(masks), width)
    vecs = [margin] + [move(margin, gmask(k)) for k in range(1, groups)]
    grad, loss = grad_hidden(ids, pairs, total, hidden, tgt, gain, vecs, width)

    grad_rows = grad.reshape(4 * L, -1)
    other = None
    for half in range(2):
        if split == 2:
            leaving = grad_rows[2 * L * half : 2 * L * (half + 1)]
            other = swap_x(leaving if half == 0 else after(leaving, other))
            acc = back_mm(grad_rows, half, wo_keep, None)
            keep, send = back_mm(other, None, wo_send, acc)
        else:
            acc = jnp.zeros((2 * L, heads), F32)
            keep, send = back_mm(grad_rows, half, wo_keep, acc)
        rs = move(send if half == 0 else after(send, r2), 1)
        if half == 0:
            over = (keep + rs.astype(F32)).astype(BF16)
            r2 = move(over, near_z)
    outer, mid = attend_back(keep, rs, r2, low, qo, vo, cosine, sine, saved)

    rows_each = width // tensor_size
    if split == 2:
        mids = [mid, swap_x(mid)]
    elif tensor_size == 1:
        mids = [mid]
    else:
        gathered = lax.all_gather(mid, "tensor", axis=0, tiled=False)
        mids = [gathered[i] for i in range(tensor_size)]
    scal = jnp.stack([x, me & 1]).astype(jnp.int32)
    away, current = adapter_products(scal, pol_states, mids, outer, rows_each)
    current = current + move(away, 1).astype(F32)
    top = fsdp_size // 2
    g = (me // 2) % groups
    rows = current.shape[0] // groups
    pieces = [
        lax.dynamic_slice_in_dim(current, (g ^ k) * rows, rows, 0) for k in range(groups)
    ]
    current = pieces[0]
    for k in range(1, groups):
        current = current + move(pieces[k].astype(BF16), k << 1).astype(F32)
    rows //= 2
    high = me // top
    away = lax.dynamic_slice_in_dim(current, (1 - high) * rows, rows, 0).astype(BF16)
    current = lax.dynamic_slice_in_dim(current, high * rows, rows, 0)
    current = (current + move(away, top).astype(F32)).astype(BF16)

    def join(bit, own, other):
        return jnp.where(
            bit == 0, jnp.concatenate([own, other], 0), jnp.concatenate([other, own], 0)
        )

    current = join(high, current, move(current, top))
    pieces = [current] + [move(current, k << 1) for k in range(1, groups)]
    step = 1
    while step < groups:
        odd = (g & step) != 0
        pieces = [jnp.where(odd, pieces[k ^ step], pieces[k]) for k in range(groups)]
        step *= 2
    current = jnp.concatenate(pieces, 0)
    grads = assemble(
        (me & 1).reshape(1), current, move(current, 1), rows_each, qo.shape[1], vo.shape[1]
    )
    return (loss[0, 0], grads[0].T, grads[1], grads[2].T, grads[3])


def solution(mesh):
    in_specs = (
        P("fsdp", None),
        P("fsdp", None),
        P("fsdp", None),
        P(),
        P("fsdp", "tensor"),
        P("fsdp", "tensor"),
        P("fsdp", "tensor"),
        P("tensor", "fsdp"),
        P(),
        P(None, "tensor"),
        P(),
        P(None, "tensor"),
        P("fsdp"),
        P(),
    )
    out_specs = (P(), P("tensor", None), P(None, "tensor"), P("tensor", None), P(None, "tensor"))
    body = functools.partial(per_device, mesh.shape["fsdp"], mesh.shape["tensor"])
    return jax.shard_map(body, mesh=mesh, in_specs=in_specs, out_specs=out_specs, check_vma=False)
```

profile of v0, /device:TPU:0, one launch (start us, length us, event | category | flops | bytes accessed | tf_op | source)
XLA Modules:
  0.0 455.2 jit_solution(1956602581201908120)
XLA Ops:
  17.8 16.7 %collective-permute-done = bf16[1,128,2048]{2,1,0:T(8,128)(2,1)} collective-permute-done((bf16[1,128,2048]{2,1,0:T(8,128)(2,1)S(1)}, bf16[1,128,2048]{2,1,0:T(8,128)(2,1)}, u32[]{:S(2)}, u32[]{:S(2)}) %collective-permute-start) | collective-permute-done | bytes 524320 | tf_op jit(solution)/shard_map/ppermute | solution.py:669
  36.5 14.8 %collective-permute-done.3 = bf16[1,128,2048]{2,1,0:T(8,128)(2,1)} collective-permute-done((bf16[1,128,2048]{2,1,0:T(8,128)(2,1)}, bf16[1,128,2048]{2,1,0:T(8,128)(2,1)}, u32[]{:S(2)}, u32[]{:S(2)}) %collective-permute-start.3) | collective-permute-done | bytes 524320 | tf_op jit(solution)/shard_map/ppermute | solution.py:669
  61.8 4.1 collective-permute-done.4
  68.1 23.2 %collective-permute-done.8.refs_2_ = bf16[512,768]{1,0:T(8,128)(2,1)S(1)} collective-permute-done((bf16[512,768]{1,0:T(8,128)(2,1)S(1)}, bf16[512,768]{1,0:T(8,128)(2,1)S(1)}, u32[]{:S(2)}, u32[]{:S(2)}) %collective-permute-start.8) | collective-permute-done | bytes 786464 | tf_op jit(solution)/shard_map/ppermute | solution.py:669
  92.7 3.6 shard_map.175
  99.3 3.5 shard_map.174
  105.0 3.8 collective-permute-start.13
  109.6 24.9 %collective-permute-done.15.refs_2_ = bf16[512,768]{1,0:T(8,128)(2,1)S(1)} collective-permute-done((bf16[512,768]{1,0:T(8,128)(2,1)S(1)}, bf16[512,768]{1,0:T(8,128)(2,1)S(1)}, u32[]{:S(2)}, u32[]{:S(2)}) %collective-permute-start.15) | collective-permute-done | bytes 786464 | tf_op jit(solution)/shard_map/ppermute | solution.py:669
  139.7 3.6 shard_map.178
  145.1 3.6 shard_map.179
  154.2 23.3 %collective-permute-done.20.refs_4_ = bf16[256,512]{1,0:T(8,128)(2,1)S(1)} collective-permute-done((bf16[256,512]{1,0:T(8,128)(2,1)S(1)}, bf16[256,512]{1,0:T(8,128)(2,1)S(1)}, u32[]{:S(2)}, u32[]{:S(2)}) %collective-permute-start.20) | collective-permute-done | bytes 262176 | tf_op jit(solution)/shard_map/ppermute | solution.py:669
  194.2 9.0 %collective-permute-done.29.refs_5_ = bf16[256,512]{1,0:T(8,128)(2,1)S(1)} collective-permute-done((bf16[256,512]{1,0:T(8,128)(2,1)S(1)}, bf16[256,512]{1,0:T(8,128)(2,1)S(1)}, u32[]{:S(2)}, u32[]{:S(2)}) %collective-permute-start.29) | collective-permute-done | bytes 262176 | tf_op jit(solution)/shard_map/ppermute | solution.py:669
  205.8 4.0 collective-permute-done.32.refs_12_.refs_4_
  213.4 8.1 %collective-permute-done.31.refs_3_ = bf16[512,768]{1,0:T(8,128)(2,1)} collective-permute-done((bf16[512,768]{1,0:T(8,128)(2,1)}, bf16[512,768]{1,0:T(8,128)(2,1)}, u32[]{:S(2)}, u32[]{:S(2)}) %collective-permute-start.31) | collective-permute-done | bytes 786464 | tf_op jit(solution)/shard_map/ppermute | solution.py:669
  224.9 3.6 shard_map.186
  229.3 3.8 shard_map.187
  238.1 7.0 %collective-permute-done.38.refs_6_ = bf16[256,512]{1,0:T(8,128)(2,1)S(1)} collective-permute-done((bf16[256,512]{1,0:T(8,128)(2,1)S(1)}, bf16[256,512]{1,0:T(8,128)(2,1)S(1)}, u32[]{:S(2)}, u32[]{:S(2)}) %collective-permute-start.38) | collective-permute-done | bytes 262176 | tf_op jit(solution)/shard_map/ppermute | solution.py:669
  247.6 8.4 %collective-permute-done.39 = bf16[256,768]{1,0:T(8,128)(2,1)S(1)} collective-permute-done((bf16[256,768]{1,0:T(8,128)(2,1)S(1)}, bf16[256,768]{1,0:T(8,128)(2,1)S(1)}, u32[]{:S(2)}, u32[]{:S(2)}) %collective-permute-start.39) | collective-permute-done | bytes 393248 | tf_op jit(solution)/shard_map/ppermute | solution.py:669
  258.4 14.6 %collective-permute-done.44.refs_7_ = bf16[256,512]{1,0:T(8,128)(2,1)S(1)} collective-permute-done((bf16[256,512]{1,0:T(8,128)(2,1)S(1)}, bf16[256,512]{1,0:T(8,128)(2,1)S(1)}, u32[]{:S(2)}, u32[]{:S(2)}) %collective-permute-start.44) | collective-permute-done | bytes 262176 | tf_op jit(solution)/shard_map/ppermute | solution.py:669
  279.9 8.0 %collective-permute-done.58.refs_15_.refs_7_ = bf16[1024,256]{1,0:T(8,128)(2,1)S(1)} collective-permute-done((bf16[1024,256]{1,0:T(8,128)(2,1)S(1)}, bf16[1024,256]{1,0:T(8,128)(2,1)S(1)}, u32[]{:S(2)}, u32[]{:S(2)}) %collective-permute-start.58) | collective-permute-done | bytes 524320 | tf_op jit(solution)/shard_map/ppermute | solution.py:669
  287.9 3.6 shard_map.193
  294.0 5.2 %collective-permute-done.51.refs_15_.refs_3_ = bf16[1024,256]{1,0:T(8,128)(2,1)S(1)} collective-permute-done((bf16[1024,256]{1,0:T(8,128)(2,1)S(1)}, bf16[1024,256]{1,0:T(8,128)(2,1)S(1)}, u32[]{:S(2)}, u32[]{:S(2)}) %collective-permute-start.51) | collective-permute-done | bytes 524320 | tf_op jit(solution)/shard_map/ppermute | solution.py:669
  302.2 8.2 %collective-permute-done.53.refs_12_.refs_6_ = bf16[1024,256]{1,0:T(8,128)(2,1)S(1)} collective-permute-done((bf16[1024,256]{1,0:T(8,128)(2,1)S(1)}, bf16[1024,256]{1,0:T(8,128)(2,1)S(1)}, u32[]{:S(2)}, u32[]{:S(2)}) %collective-permute-start.53) | collective-permute-done | bytes 524320 | tf_op jit(solution)/shard_map/ppermute | solution.py:669
  310.4 10.8 %collective-permute-done.54.refs_13_.refs_7_ = bf16[1024,256]{1,0:T(8,128)(2,1)S(1)} collective-permute-done((bf16[1024,256]{1,0:T(8,128)(2,1)S(1)}, bf16[1024,256]{1,0:T(8,128)(2,1)S(1)}, u32[]{:S(2)}, u32[]{:S(2)}) %collective-permute-start.54) | collective-permute-done | bytes 524320 | tf_op jit(solution)/shard_map/ppermute | solution.py:669
  350.0 3.5 collective-permute-done.69.refs_3_
  362.1 9.7 %collective-permute-done.70.x_ref = bf16[256,1024]{1,0:T(8,128)(2,1)S(1)} collective-permute-done((bf16[256,1024]{1,0:T(8,128)(2,1)S(1)}, bf16[256,1024]{1,0:T(8,128)(2,1)S(1)}, u32[]{:S(2)}, u32[]{:S(2)}) %collective-permute-start.70) | collective-permute-done | bytes 524320 | tf_op jit(solution)/shard_map/ppermute | solution.py:672
  379.6 9.7 %collective-permute-done.71.x_ref = bf16[256,1024]{1,0:T(8,128)(2,1)S(1)} collective-permute-done((bf16[256,1024]{1,0:T(8,128)(2,1)S(1)}, bf16[256,1024]{1,0:T(8,128)(2,1)S(1)}, u32[]{:S(2)}, u32[]{:S(2)}) %collective-permute-start.71) | collective-permute-done | bytes 524320 | tf_op jit(solution)/shard_map/ppermute | solution.py:672
  389.4 3.8 shard_map.198
  419.7 4.7 %collective-permute-done.79 = bf16[16,5376]{1,0:T(8,128)(2,1)S(1)} collective-permute-done((bf16[16,5376]{1,0:T(8,128)(2,1)S(1)}, bf16[16,5376]{1,0:T(8,128)(2,1)S(1)}, u32[]{:S(2)}, u32[]{:S(2)}) %collective-permute-start.79) | collective-permute-done | bytes 172064 | tf_op jit(solution)/shard_map/ppermute | solution.py:669
  427.7 6.8 %collective-permute-done.80 = bf16[8,5376]{1,0:T(8,128)(2,1)S(1)} collective-permute-done((bf16[8,5376]{1,0:T(8,128)(2,1)S(1)}, bf16[8,5376]{1,0:T(8,128)(2,1)S(1)}, u32[]{:S(2)}, u32[]{:S(2)}) %collective-permute-start.80) | collective-permute-done | bytes 86048 | tf_op jit(solution)/shard_map/ppermute | solution.py:669
  434.6 5.9 %collective-permute-done.81 = bf16[8,5376]{1,0:T(8,128)(2,1)S(1)} collective-permute-done((bf16[8,5376]{1,0:T(8,128)(2,1)S(1)}, bf16[8,5376]{1,0:T(8,128)(2,1)S(1)}, u32[]{:S(2)}, u32[]{:S(2)}) %collective-permute-start.81) | collective-permute-done | bytes 86048 | tf_op jit(solution)/shard_map/ppermute | solution.py:669
  444.0 4.7 %collective-permute-done.82 = bf16[16,5376]{1,0:T(8,128)(2,1)S(1)} collective-permute-done((bf16[16,5376]{1,0:T(8,128)(2,1)S(1)}, bf16[16,5376]{1,0:T(8,128)(2,1)S(1)}, u32[]{:S(2)}, u32[]{:S(2)}) %collective-permute-start.82) | collective-permute-done | bytes 172064 | tf_op jit(solution)/shard_map/ppermute | solution.py:669
  (506 shorter events, 183.7 us)
Async XLA Ops:
  8.8 25.7 %collective-permute-start = (bf16[1,128,2048]{2,1,0:T(8,128)(2,1)S(1)}, bf16[1,128,2048]{2,1,0:T(8,128)(2,1)}, u32[]{:S(2)}, u32[]{:S(2)}) collective-permute-start(bf16[1,128,2048]{2,1,0:T(8,128)(2,1)S(1)} %get-tuple-element.108), channel_id=1, source_target_pairs={{0,8},{2,10},{4,12},{6,14},{8,0},{10,2},{12,4},{14,6},{16,24},{18,... | collective-permute-start | bytes 1572872 | tf_op jit(solution)/shard_map/ppermute | solution.py:669
  12.0 40.8 %collective-permute-start.5 = (bf16[512,768]{1,0:T(8,128)(2,1)S(1)}, bf16[512,768]{1,0:T(8,128)(2,1)S(1)}, u32[]{:S(2)}, u32[]{:S(2)}) collective-permute-start(bf16[512,768]{1,0:T(8,128)(2,1)S(1)} %pad_maximum_fusion.1.refs_0_), channel_id=1, source_target_pairs={{0,4},{2,6},{4,0},{6,2},{8,12},{10,14},{12,8},{14,10},{16,20},{18,... | collective-permute-start | bytes 2359304 | tf_op jit(solution)/shard_map/ppermute | solution.py:669
  13.6 40.1 %collective-permute-start.6 = (bf16[512,768]{1,0:T(8,128)(2,1)S(1)}, bf16[512,768]{1,0:T(8,128)(2,1)}, u32[]{:S(2)}, u32[]{:S(2)}) collective-permute-start(bf16[512,768]{1,0:T(8,128)(2,1)S(1)} %pad_maximum_fusion.1.refs_0_), channel_id=1, source_target_pairs={{0,16},{2,18},{4,20},{6,22},{8,24},{10,26},{12,28},{14,30},{16,0},... | collective-permute-start | bytes 2359304 | tf_op jit(solution)/shard_map/ppermute | solution.py:669
  16.2 44.5 %collective-permute-start.2 = (bf16[2,128,2048]{2,1,0:T(8,128)(2,1)}, bf16[2,128,2048]{2,1,0:T(8,128)(2,1)}, u32[]{:S(2)}, u32[]{:S(2)}) collective-permute-start(bf16[2,128,2048]{2,1,0:T(8,128)(2,1)} %get-tuple-element.109), channel_id=1, source_target_pairs={{0,2},{2,0},{4,6},{6,4},{8,10},{10,8},{12,14},{14,12},{16,18},{18,... | collective-permute-start | bytes 3145736 | tf_op jit(solution)/shard_map/ppermute | solution.py:669
  16.2 35.1 %collective-permute-start.3 = (bf16[1,128,2048]{2,1,0:T(8,128)(2,1)}, bf16[1,128,2048]{2,1,0:T(8,128)(2,1)}, u32[]{:S(2)}, u32[]{:S(2)}) collective-permute-start(bf16[1,128,2048]{2,1,0:T(8,128)(2,1)} %get-tuple-element.110), channel_id=1, source_target_pairs={{0,10},{2,8},{4,14},{6,12},{8,2},{10,0},{12,6},{14,4},{16,26},{18,... | collective-permute-start | bytes 1572872 | tf_op jit(solution)/shard_map/ppermute | solution.py:669
  34.5 23.3 %collective-permute-start.1 = (bf16[1,128,2048]{2,1,0:T(8,128)(2,1)}, bf16[1,128,2048]{2,1,0:T(8,128)(2,1)}, u32[]{:S(2)}, u32[]{:S(2)}) collective-permute-start(bf16[1,128,2048]{2,1,0:T(8,128)(2,1)} %collective-permute-done), channel_id=1, source_target_pairs={{0,1},{1,0},{2,3},{3,2},{4,5},{5,4},{6,7},{7,6},{8,9},{9,8},{10,11... | collective-permute-start | bytes 1572872 | tf_op jit(solution)/shard_map/ppermute | solution.py:672
  53.7 37.6 %collective-permute-start.8 = (bf16[512,768]{1,0:T(8,128)(2,1)S(1)}, bf16[512,768]{1,0:T(8,128)(2,1)S(1)}, u32[]{:S(2)}, u32[]{:S(2)}) collective-permute-start(bf16[512,768]{1,0:T(8,128)(2,1)S(1)} %pad_maximum_fusion.2.refs_0_), channel_id=1, source_target_pairs={{0,16},{2,18},{4,20},{6,22},{8,24},{10,26},{12,28},{14,30},{16,0},... | collective-permute-start | bytes 2359304 | tf_op jit(solution)/shard_map/ppermute | solution.py:669
  56.2 35.1 %collective-permute-start.9 = (bf16[512,768]{1,0:T(8,128)(2,1)S(1)}, bf16[512,768]{1,0:T(8,128)(2,1)S(1)}, u32[]{:S(2)}, u32[]{:S(2)}) collective-permute-start(bf16[512,768]{1,0:T(8,128)(2,1)S(1)} %pad_maximum_fusion.2.refs_0_), channel_id=1, source_target_pairs={{0,4},{2,6},{4,0},{6,2},{8,12},{10,14},{12,8},{14,10},{16,20},{18,... | collective-permute-start | bytes 2359304 | tf_op jit(solution)/shard_map/ppermute | solution.py:669
  57.8 35.0 %collective-permute-start.7 = (bf16[512,768]{1,0:T(8,128)(2,1)}, bf16[512,768]{1,0:T(8,128)(2,1)S(1)}, u32[]{:S(2)}, u32[]{:S(2)}) collective-permute-start(bf16[512,768]{1,0:T(8,128)(2,1)} %collective-permute-done.6.refs_2_), channel_id=1, source_target_pairs={{0,4},{2,6},{4,0},{6,2},{8,12},{10,14},{12,8},{14,10},{16,20},{18,... | collective-permute-start | bytes 2359304 | tf_op jit(solution)/shard_map/ppermute | solution.py:669
  97.1 37.4 %collective-permute-start.15 = (bf16[512,768]{1,0:T(8,128)(2,1)S(1)}, bf16[512,768]{1,0:T(8,128)(2,1)S(1)}, u32[]{:S(2)}, u32[]{:S(2)}) collective-permute-start(bf16[512,768]{1,0:T(8,128)(2,1)S(1)} %pad_maximum_fusion.4.refs_0_), channel_id=1, source_target_pairs={{0,16},{2,18},{4,20},{6,22},{8,24},{10,26},{12,28},{14,30},{16,0},... | collective-permute-start | bytes 2359304 | tf_op jit(solution)/shard_map/ppermute | solution.py:669
  97.3 37.2 %collective-permute-start.16 = (bf16[512,768]{1,0:T(8,128)(2,1)S(1)}, bf16[512,768]{1,0:T(8,128)(2,1)S(1)}, u32[]{:S(2)}, u32[]{:S(2)}) collective-permute-start(bf16[512,768]{1,0:T(8,128)(2,1)S(1)} %pad_maximum_fusion.4.refs_0_), channel_id=1, source_target_pairs={{0,4},{2,6},{4,0},{6,2},{8,12},{10,14},{12,8},{14,10},{16,20},{18,... | collective-permute-start | bytes 2359304 | tf_op jit(solution)/shard_map/ppermute | solution.py:669
  98.8 38.6 %collective-permute-start.14 = (bf16[512,768]{1,0:T(8,128)(2,1)S(1)}, bf16[512,768]{1,0:T(8,128)(2,1)}, u32[]{:S(2)}, u32[]{:S(2)}) collective-permute-start(bf16[512,768]{1,0:T(8,128)(2,1)S(1)} %collective-permute-done.8.refs_2_), channel_id=1, source_target_pairs={{0,4},{2,6},{4,0},{6,2},{8,12},{10,14},{12,8},{14,10},{16,20},{18,... | collective-permute-start | bytes 2359304 | tf_op jit(solution)/shard_map/ppermute | solution.py:669
  105.0 43.7 %collective-permute-start.13 = (bf16[256,768]{1,0:T(8,128)(2,1)}, bf16[256,768]{1,0:T(8,128)(2,1)}, u32[]{:S(2)}, u32[]{:S(2)}) collective-permute-start(bf16[256,768]{1,0:T(8,128)(2,1)} %pad_maximum_fusion.10), channel_id=1, source_target_pairs={{0,8},{2,10},{4,12},{6,14},{8,0},{10,2},{12,4},{14,6},{16,24},{18,... | collective-permute-start | bytes 1179656 | tf_op jit(solution)/shard_map/ppermute | solution.py:669
  135.8 42.5 %collective-permute-start.23 = (bf16[512,768]{1,0:T(8,128)(2,1)S(1)}, bf16[512,768]{1,0:T(8,128)(2,1)}, u32[]{:S(2)}, u32[]{:S(2)}) collective-permute-start(bf16[512,768]{1,0:T(8,128)(2,1)S(1)} %pad_maximum_fusion.3.refs_0_), channel_id=1, source_target_pairs={{0,16},{2,18},{4,20},{6,22},{8,24},{10,26},{12,28},{14,30},{16,0},... | collective-permute-start | bytes 2359304 | tf_op jit(solution)/shard_map/ppermute | solution.py:669
  135.9 42.4 %collective-permute-start.24 = (bf16[512,768]{1,0:T(8,128)(2,1)S(1)}, bf16[512,768]{1,0:T(8,128)(2,1)S(1)}, u32[]{:S(2)}, u32[]{:S(2)}) collective-permute-start(bf16[512,768]{1,0:T(8,128)(2,1)S(1)} %pad_maximum_fusion.3.refs_0_), channel_id=1, source_target_pairs={{0,4},{2,6},{4,0},{6,2},{8,12},{10,14},{12,8},{14,10},{16,20},{18,... | collective-permute-start | bytes 2359304 | tf_op jit(solution)/shard_map/ppermute | solution.py:669
  148.8 30.1 %collective-permute-start.22 = (bf16[512,768]{1,0:T(8,128)(2,1)S(1)}, bf16[512,768]{1,0:T(8,128)(2,1)S(1)}, u32[]{:S(2)}, u32[]{:S(2)}) collective-permute-start(bf16[512,768]{1,0:T(8,128)(2,1)S(1)} %copy-done.50), channel_id=1, source_target_pairs={{0,4},{2,6},{4,0},{6,2},{8,12},{10,14},{12,8},{14,10},{16,20},{18,... | collective-permute-start | bytes 2359304 | tf_op jit(solution)/shard_map/ppermute | solution.py:669
  152.6 24.9 %collective-permute-start.20 = (bf16[256,512]{1,0:T(8,128)(2,1)S(1)}, bf16[256,512]{1,0:T(8,128)(2,1)S(1)}, u32[]{:S(2)}, u32[]{:S(2)}) collective-permute-start(bf16[256,512]{1,0:T(8,128)(2,1)S(1)} %pad_maximum_fusion.14.refs_0_), channel_id=1, source_target_pairs={{0,8},{2,10},{4,12},{6,14},{8,0},{10,2},{12,4},{14,6},{16,24},{18,... | collective-permute-start | bytes 786440 | tf_op jit(solution)/shard_map/ppermute | solution.py:669
  183.3 26.5 %collective-permute-start.32 = (bf16[1024,256]{1,0:T(8,128)(2,1)S(1)}, bf16[1024,256]{1,0:T(8,128)(2,1)}, u32[]{:S(2)}, u32[]{:S(2)}) collective-permute-start(bf16[1024,256]{1,0:T(8,128)(2,1)S(1)} %constant_dynamic-slice_fusion.1.refs_12_.refs_0_), channel_id=1, source_target_pairs={{0,16},{2,18},{4,20},{6,22},{8,24},{10,26},{12,28},{14,30},{16,0},... | collective-permute-start | bytes 1572872 | tf_op jit(solution)/shard_map/ppermute | solution.py:669
  189.8 20.0 %collective-permute-start.33 = (bf16[1024,256]{1,0:T(8,128)(2,1)S(1)}, bf16[1024,256]{1,0:T(8,128)(2,1)S(1)}, u32[]{:S(2)}, u32[]{:S(2)}) collective-permute-start(bf16[1024,256]{1,0:T(8,128)(2,1)S(1)} %constant_dynamic-slice_fusion.1.refs_12_.refs_0_), channel_id=1, source_target_pairs={{0,4},{2,6},{4,0},{6,2},{8,12},{10,14},{12,8},{14,10},{16,20},{18,... | collective-permute-start | bytes 1572872 | tf_op jit(solution)/shard_map/ppermute | solution.py:669
  191.8 29.8 %collective-permute-start.31 = (bf16[512,768]{1,0:T(8,128)(2,1)}, bf16[512,768]{1,0:T(8,128)(2,1)}, u32[]{:S(2)}, u32[]{:S(2)}) collective-permute-start(bf16[512,768]{1,0:T(8,128)(2,1)} %collective-permute-done.23.refs_2_), channel_id=1, source_target_pairs={{0,4},{2,6},{4,0},{6,2},{8,12},{10,14},{12,8},{14,10},{16,20},{18,... | collective-permute-start | bytes 2359304 | tf_op jit(solution)/shard_map/ppermute | solution.py:669
  203.2 29.9 %collective-permute-start.30 = (bf16[256,768]{1,0:T(8,128)(2,1)}, bf16[256,768]{1,0:T(8,128)(2,1)}, u32[]{:S(2)}, u32[]{:S(2)}) collective-permute-start(bf16[256,768]{1,0:T(8,128)(2,1)} %pad_maximum_fusion.12), channel_id=1, source_target_pairs={{0,8},{2,10},{4,12},{6,14},{8,0},{10,2},{12,4},{14,6},{16,24},{18,... | collective-permute-start | bytes 1179656 | tf_op jit(solution)/shard_map/ppermute | solution.py:669
  210.6 34.5 %collective-permute-start.40 = (bf16[1024,256]{1,0:T(8,128)(2,1)S(1)}, bf16[1024,256]{1,0:T(8,128)(2,1)S(1)}, u32[]{:S(2)}, u32[]{:S(2)}) collective-permute-start(bf16[1024,256]{1,0:T(8,128)(2,1)S(1)} %constant_dynamic-slice_fusion.3.refs_13_.refs_1_), channel_id=1, source_target_pairs={{0,16},{2,18},{4,20},{6,22},{8,24},{10,26},{12,28},{14,30},{16,0},... | collective-permute-start | bytes 1572872 | tf_op jit(solution)/shard_map/ppermute | solution.py:669
  210.6 34.6 %collective-permute-start.41 = (bf16[1024,256]{1,0:T(8,128)(2,1)S(1)}, bf16[1024,256]{1,0:T(8,128)(2,1)S(1)}, u32[]{:S(2)}, u32[]{:S(2)}) collective-permute-start(bf16[1024,256]{1,0:T(8,128)(2,1)S(1)} %constant_dynamic-slice_fusion.3.refs_13_.refs_1_), channel_id=1, source_target_pairs={{0,4},{2,6},{4,0},{6,2},{8,12},{10,14},{12,8},{14,10},{16,20},{18,... | collective-permute-start | bytes 1572872 | tf_op jit(solution)/shard_map/ppermute | solution.py:669
  236.0 19.9 %collective-permute-start.39 = (bf16[256,768]{1,0:T(8,128)(2,1)S(1)}, bf16[256,768]{1,0:T(8,128)(2,1)S(1)}, u32[]{:S(2)}, u32[]{:S(2)}) collective-permute-start(bf16[256,768]{1,0:T(8,128)(2,1)S(1)} %pad_maximum_fusion.13), channel_id=1, source_target_pairs={{0,8},{2,10},{4,12},{6,14},{8,0},{10,2},{12,4},{14,6},{16,24},{18,... | collective-permute-start | bytes 1179656 | tf_op jit(solution)/shard_map/ppermute | solution.py:669
  245.7 28.3 %collective-permute-start.49 = (bf16[1024,256]{1,0:T(8,128)(2,1)S(1)}, bf16[1024,256]{1,0:T(8,128)(2,1)S(1)}, u32[]{:S(2)}, u32[]{:S(2)}) collective-permute-start(bf16[1024,256]{1,0:T(8,128)(2,1)S(1)} %get-tuple-element.178.refs_12_.refs_0_), channel_id=1, source_target_pairs={{0,4},{2,6},{4,0},{6,2},{8,12},{10,14},{12,8},{14,10},{16,20},{18,... | collective-permute-start | bytes 1572872 | tf_op jit(solution)/shard_map/ppermute | solution.py:669
  246.5 27.5 %collective-permute-start.50 = (bf16[1024,256]{1,0:T(8,128)(2,1)S(1)}, bf16[1024,256]{1,0:T(8,128)(2,1)S(1)}, u32[]{:S(2)}, u32[]{:S(2)}) collective-permute-start(bf16[1024,256]{1,0:T(8,128)(2,1)S(1)} %get-tuple-element.178.refs_12_.refs_0_), channel_id=1, source_target_pairs={{0,16},{2,18},{4,20},{6,22},{8,24},{10,26},{12,28},{14,30},{16,0},... | collective-permute-start | bytes 1572872 | tf_op jit(solution)/shard_map/ppermute | solution.py:669
  257.3 22.6 %collective-permute-start.57 = (bf16[1024,256]{1,0:T(8,128)(2,1)}, bf16[1024,256]{1,0:T(8,128)(2,1)S(1)}, u32[]{:S(2)}, u32[]{:S(2)}) collective-permute-start(bf16[1024,256]{1,0:T(8,128)(2,1)} %collective-permute-done.32.refs_12_.refs_4_), channel_id=1, source_target_pairs={{0,4},{2,6},{4,0},{6,2},{8,12},{10,14},{12,8},{14,10},{16,20},{18,... | collective-permute-start | bytes 1572872 | tf_op jit(solution)/shard_map/ppermute | solution.py:669
  274.3 24.9 %collective-permute-start.51 = (bf16[1024,256]{1,0:T(8,128)(2,1)S(1)}, bf16[1024,256]{1,0:T(8,128)(2,1)S(1)}, u32[]{:S(2)}, u32[]{:S(2)}) collective-permute-start(bf16[1024,256]{1,0:T(8,128)(2,1)S(1)} %get-tuple-element.179.refs_13_.refs_1_), channel_id=1, source_target_pairs={{0,4},{2,6},{4,0},{6,2},{8,12},{10,14},{12,8},{14,10},{16,20},{18,... | collective-permute-start | bytes 1572872 | tf_op jit(solution)/shard_map/ppermute | solution.py:669
  275.5 25.8 %collective-permute-start.52 = (bf16[1024,256]{1,0:T(8,128)(2,1)S(1)}, bf16[1024,256]{1,0:T(8,128)(2,1)S(1)}, u32[]{:S(2)}, u32[]{:S(2)}) collective-permute-start(bf16[1024,256]{1,0:T(8,128)(2,1)S(1)} %get-tuple-element.179.refs_13_.refs_1_), channel_id=1, source_target_pairs={{0,16},{2,18},{4,20},{6,22},{8,24},{10,26},{12,28},{14,30},{16,0},... | collective-permute-start | bytes 1572872 | tf_op jit(solution)/shard_map/ppermute | solution.py:669
  278.3 50.9 %collective-permute-start.56 = (bf16[2,1024,256]{2,1,0:T(8,128)(2,1)S(1)}, bf16[2,1024,256]{2,1,0:T(8,128)(2,1)S(1)}, u32[]{:S(2)}, u32[]{:S(2)}) collective-permute-start(bf16[2,1024,256]{2,1,0:T(8,128)(2,1)S(1)} %shard_map.192), channel_id=1, source_target_pairs={{0,1},{1,0},{2,3},{3,2},{4,5},{5,4},{6,7},{7,6},{8,9},{9,8},{10,11... | collective-permute-start | bytes 3145736 | tf_op jit(solution)/shard_map/ppermute | solution.py:672
  291.5 37.7 %collective-permute-start.59 = (bf16[2,1024,256]{2,1,0:T(8,128)(2,1)S(1)}, bf16[2,1024,256]{2,1,0:T(8,128)(2,1)S(1)}, u32[]{:S(2)}, u32[]{:S(2)}) collective-permute-start(bf16[2,1024,256]{2,1,0:T(8,128)(2,1)S(1)} %shard_map.193), channel_id=1, source_target_pairs={{0,1},{1,0},{2,3},{3,2},{4,5},{5,4},{6,7},{7,6},{8,9},{9,8},{10,11... | collective-permute-start | bytes 3145736 | tf_op jit(solution)/shard_map/ppermute | solution.py:672
  302.2 24.5 %collective-permute-start.48 = (bf16[128,1024]{1,0:T(8,128)(2,1)S(1)}, bf16[128,1024]{1,0:T(8,128)(2,1)S(1)}, u32[]{:S(2)}, u32[]{:S(2)}) collective-permute-start(bf16[128,1024]{1,0:T(8,128)(2,1)S(1)} %copy-done.111), channel_id=1, source_target_pairs={{0,10},{2,8},{4,14},{6,12},{8,2},{10,0},{12,6},{14,4},{16,26},{18,... | collective-permute-start | bytes 786440 | tf_op jit(solution)/shard_map/ppermute | solution.py:669
  (191 other events, 1807.0 us)
where the time goes:
time: 457 us; the launch traced here: 455 us
  waiting for transfers between devices  262 us (57%)
  starting transfers between devices  72.1 us (16%)
  Pallas kernels  68.1 us (15%)
  local copies, waits for them, and re-layouts  37.9 us (8%)
  other arithmetic  10.6 us (2%)
    ppermute x72, waiting for transfers between devices, move(): lax.ppermute(value, 'fsdp', [(i, i ^ mask) for i in range(fsdp_size)])  234 us
    ppermute x72, starting transfers between devices, move(): lax.ppermute(value, 'fsdp', [(i, i ^ mask) for i in range(fsdp_size)])  57.4 us
    unnamed x254, local copies, waits for them, and re-layouts  33.4 us
    ppermute x7, waiting for transfers between devices, swap_x(): return lax.ppermute(value, 'tensor', [(0, 1), (1, 0)])  26.9 us
    pallas_call x8, Pallas kernels, mm(): pl.pallas_call(functools.partial(mm_body, len(ws)), grid=(cols // tile,),...  26.7 us
    pallas_call x4, Pallas kernels, back_mm(): pl.pallas_call(functools.partial(back_body, tuple((len(w) for w in ws)),...  11.2 us
    pallas_call x4, Pallas kernels, out_mm(): pl.pallas_call(functools.partial(out_body, n, len(parts), tuple((len(w) f...  10.6 us
  transfers between devices with their start and end apart: 86, of which 40 were waited for; matrix products, arithmetic and copies ran while one was open for 3% of the time, Pallas kernels for 10%

commit v1 on v0

--- a/solution.py
+++ b/solution.py
@@ -80,22 +80,30 @@
                 go[:, j * part : (j + 1) * part] = gain[:, src]
 
 
-def prep(idx, ref, pol, tgt, gain, parts, part, split, marks=()):
+def prep(idx, ref, pol, tgt, gain, parts, part, split):
     tokens = ref.shape[0]
     xs = lambda n: jax.ShapeDtypeStruct((n, tokens, parts * part), BF16)
     far = 1 if split == 2 else 2
     width = parts // split * part
+    tile = 32
     shapes = [xs(2), xs(2), xs(far), xs(far)]
     shapes += [jax.ShapeDtypeStruct((tokens, width), BF16)] * 4
     shapes += [jax.ShapeDtypeStruct((1, width), F32)]
     return pl.pallas_call(
         functools.partial(prep_body, parts, part, split),
-        in_specs=[smem()] + [pl.BlockSpec(memory_space=pltpu.VMEM)] * (4 + len(marks)),
-        out_specs=[pl.BlockSpec(memory_space=pltpu.VMEM)] * 9,
+        grid=(tokens // tile,),
+        in_specs=[smem()]
+        + [pl.BlockSpec((tile, a.shape[1]), lambda i: (i, 0)) for a in (ref, pol, tgt)]
+        + [full(gain)],
+        out_specs=[
+            pl.BlockSpec((a.shape[0], tile, a.shape[2]), lambda i: (0, i, 0)) for a in shapes[:4]
+        ]
+        + [pl.BlockSpec((tile, width), lambda i: (i, 0))] * 4
+        + [full(shapes[8])],
         out_shape=shapes,
-        compiler_params=params(32),
+        compiler_params=params(60),
         cost_estimate=SMALL,
-    )(idx, ref, pol, tgt, gain, *marks)
+    )(idx, ref, pol, tgt, gain)
 
 
 def tile_of(cols):
@@ -132,7 +140,11 @@
         out_specs=[pl.BlockSpec((rows // 2, tile), lambda i: (0, i))] * 2,
         out_shape=[jax.ShapeDtypeStruct((rows // 2, cols), out_dtype)] * 2,
         compiler_params=params(32),
-        cost_estimate=SMALL,
+        cost_estimate=pl.CostEstimate(
+            flops=2 * rows * depth * cols,
+            bytes_accessed=2 * (rows * (depth + cols) + depth * cols),
+            transcendentals=0,
+        ),
     )(x, *ws, *marks)
 
 
@@ -375,7 +387,7 @@
         in_specs=[full(a) for a in inputs],
         out_specs=[full(a) for a in shapes],
         out_shape=shapes,
-        compiler_params=params(32),
+        compiler_params=params(60),
         cost_estimate=SMALL,
     )(*inputs)
 
@@ -720,7 +732,6 @@
             idx.append((me ^ tmask(d) ^ gmask(k)) * split + side)
     idx.append(x)
     idx = jnp.stack(idx).astype(jnp.int32)
-    marks = ()
     prepared = prep(
         idx,
         ref_states,
@@ -730,7 +741,6 @@
         parts,
         part,
         split,
-        marks,
     )
     xs, ts, gain = prepared[:4], prepared[4:8], prepared[8]
     near = move(xs[1], 1)
@@ -804,6 +814,7 @@
         make_shard(2, zs[0])
     before = None
     ends = []
+    marks = ()
     for j in range(kv_local):
         if wide:
             marks = (marker(zs[j + 1], ys[j + 1]),)

time: 457 us -> 443 us (0.969)
  waiting for transfers between devices: 262 us -> 284 us
  local copies, waits for them, and re-layouts: 37.9 us -> 17.8 us
  starting transfers between devices: 72.1 us -> 60.8 us
    ppermute x72, waiting for transfers between devices: 234 us -> 254 us  [move(): lax.ppermute(value, 'fsdp', [(i, i ^ mask) for i in range(fsdp_size)])]
    unnamed x254 -> x126, local copies, waits for them, and re-layouts: 33.4 us -> 13.2 us
    ppermute x72, starting transfers between devices: 57.4 us -> 49.3 us  [move(): lax.ppermute(value, 'fsdp', [(i, i ^ mask) for i in range(fsdp_size)])]
    pallas_call x8, Pallas kernels: 26.7 us -> 22.1 us  [mm(): pl.pallas_call(functools.partial(mm_body, len(ws)), grid=(cols // tile,),...]
  transfers between devices with their start and end apart: 86 -> 86, of which waited for: 40 -> 41; matrix products, arithmetic and copies ran while one was open for 3% -> 3% of each run, Pallas kernels for 10% -> 10%
where the time goes in v1:
time: 443 us; the launch traced here: 442 us
  waiting for transfers between devices  284 us (64%)
  Pallas kernels  67.9 us (15%)
  starting transfers between devices  60.8 us (14%)
  local copies, waits for them, and re-layouts  17.8 us (4%)
  other arithmetic  6.97 us (2%)
    ppermute x72, waiting for transfers between devices, move(): lax.ppermute(value, 'fsdp', [(i, i ^ mask) for i in range(fsdp_size)])  254 us
    ppermute x72, starting transfers between devices, move(): lax.ppermute(value, 'fsdp', [(i, i ^ mask) for i in range(fsdp_size)])  49.3 us
    ppermute x7, waiting for transfers between devices, swap_x(): return lax.ppermute(value, 'tensor', [(0, 1), (1, 0)])  27.4 us
    pallas_call x8, Pallas kernels, mm(): pl.pallas_call(functools.partial(mm_body, len(ws)), grid=(cols // tile,),...  22.1 us
    unnamed x126, local copies, waits for them, and re-layouts  13.2 us
    pallas_call x4, Pallas kernels, back_mm(): pl.pallas_call(functools.partial(back_body, tuple((len(w) for w in ws)),...  9.54 us
    pallas_call x4, Pallas kernels, out_mm(): pl.pallas_call(functools.partial(out_body, n, len(parts), tuple((len(w) f...  9.38 us
  transfers between devices with their start and end apart: 86, of which 41 were waited for; matrix products, arithmetic and copies ran while one was open for 3% of the time, Pallas kernels for 10%

profile of v1, /device:TPU:0, one launch (start us, length us, event | category | flops | bytes accessed | tf_op | source)
XLA Modules:
  0.0 442.3 jit_solution(1289414796010095066)
XLA Ops:
  10.6 6.1 %shard_map.173 = (bf16[2,128,2048]{2,1,0:T(8,128)(2,1)}, bf16[2,128,2048]{2,1,0:T(8,128)(2,1)}, bf16[1,128,2048]{2,1,0:T(8,128)(2,1)}, bf16[1,128,2048]{2,1,0:T(...) custom-call(s32[49]{0:T(128)} %stack.244.idx, ...), custom_call_target="tpu_custom_call" | custom-call | flops 1 | bytes 1 | tf_op jit(solution)/shard_map/pallas_call | solution.py:92
  21.8 25.9 %collective-permute-done = bf16[1,128,2048]{2,1,0:T(8,128)(2,1)} collective-permute-done((bf16[1,128,2048]{2,1,0:T(8,128)(2,1)}, bf16[1,128,2048]{2,1,0:T(8,128)(2,1)}, u32[]{:S(2)}, u32[]{:S(2)}) %collective-permute-start) | collective-permute-done | bytes 524320 | tf_op jit(solution)/shard_map/ppermute | solution.py:681
  50.4 5.0 %collective-permute-done.3 = bf16[1,128,2048]{2,1,0:T(8,128)(2,1)} collective-permute-done((bf16[1,128,2048]{2,1,0:T(8,128)(2,1)}, bf16[1,128,2048]{2,1,0:T(8,128)(2,1)}, u32[]{:S(2)}, u32[]{:S(2)}) %collective-permute-start.3) | collective-permute-done | bytes 524320 | tf_op jit(solution)/shard_map/ppermute | solution.py:681
  64.6 4.9 %collective-permute-done.4 = bf16[1,128,2048]{2,1,0:T(8,128)(2,1)S(1)} collective-permute-done((bf16[1,128,2048]{2,1,0:T(8,128)(2,1)}, bf16[1,128,2048]{2,1,0:T(8,128)(2,1)S(1)}, u32[]{:S(2)}, u32[]{:S(2)}) %collective-permute-start.4) | collective-permute-done | bytes 524320 | tf_op jit(solution)/shard_map/ppermute | solution.py:684
  71.8 22.9 %collective-permute-done.8.refs_2_ = bf16[512,768]{1,0:T(8,128)(2,1)S(1)} collective-permute-done((bf16[512,768]{1,0:T(8,128)(2,1)S(1)}, bf16[512,768]{1,0:T(8,128)(2,1)S(1)}, u32[]{:S(2)}, u32[]{:S(2)}) %collective-permute-start.8) | collective-permute-done | bytes 786464 | tf_op jit(solution)/shard_map/ppermute | solution.py:681
  95.8 3.5 shard_map.175
  102.8 3.5 shard_map.174
  108.3 28.9 %collective-permute-done.15.refs_2_ = bf16[512,768]{1,0:T(8,128)(2,1)S(1)} collective-permute-done((bf16[512,768]{1,0:T(8,128)(2,1)S(1)}, bf16[512,768]{1,0:T(8,128)(2,1)S(1)}, u32[]{:S(2)}, u32[]{:S(2)}) %collective-permute-start.15) | collective-permute-done | bytes 786464 | tf_op jit(solution)/shard_map/ppermute | solution.py:681
  149.0 10.7 %collective-permute-done.20.refs_4_ = bf16[256,512]{1,0:T(8,128)(2,1)S(1)} collective-permute-done((bf16[256,512]{1,0:T(8,128)(2,1)S(1)}, bf16[256,512]{1,0:T(8,128)(2,1)S(1)}, u32[]{:S(2)}, u32[]{:S(2)}) %collective-permute-start.20) | collective-permute-done | bytes 262176 | tf_op jit(solution)/shard_map/ppermute | solution.py:681
  162.4 11.5 %collective-permute-done.23.refs_2_ = bf16[512,768]{1,0:T(8,128)(2,1)S(1)} collective-permute-done((bf16[512,768]{1,0:T(8,128)(2,1)S(1)}, bf16[512,768]{1,0:T(8,128)(2,1)S(1)}, u32[]{:S(2)}, u32[]{:S(2)}) %collective-permute-start.23) | collective-permute-done | bytes 786464 | tf_op jit(solution)/shard_map/ppermute | solution.py:681
  185.8 13.5 %collective-permute-done.32.refs_12_.refs_4_ = bf16[1024,256]{1,0:T(8,128)(2,1)S(1)} collective-permute-done((bf16[1024,256]{1,0:T(8,128)(2,1)S(1)}, bf16[1024,256]{1,0:T(8,128)(2,1)S(1)}, u32[]{:S(2)}, u32[]{:S(2)}) %collective-permute-start.32) | collective-permute-done | bytes 524320 | tf_op jit(solution)/shard_map/ppermute | solution.py:681
  200.0 4.5 %collective-permute-done.29.refs_5_ = bf16[256,512]{1,0:T(8,128)(2,1)S(1)} collective-permute-done((bf16[256,512]{1,0:T(8,128)(2,1)S(1)}, bf16[256,512]{1,0:T(8,128)(2,1)S(1)}, u32[]{:S(2)}, u32[]{:S(2)}) %collective-permute-start.29) | collective-permute-done | bytes 262176 | tf_op jit(solution)/shard_map/ppermute | solution.py:681
  204.7 9.3 %collective-permute-done.31.refs_3_ = bf16[512,768]{1,0:T(8,128)(2,1)S(1)} collective-permute-done((bf16[512,768]{1,0:T(8,128)(2,1)S(1)}, bf16[512,768]{1,0:T(8,128)(2,1)S(1)}, u32[]{:S(2)}, u32[]{:S(2)}) %collective-permute-start.31) | collective-permute-done | bytes 786464 | tf_op jit(solution)/shard_map/ppermute | solution.py:681
  219.2 7.1 %collective-permute-done.30 = bf16[256,768]{1,0:T(8,128)(2,1)S(1)} collective-permute-done((bf16[256,768]{1,0:T(8,128)(2,1)S(1)}, bf16[256,768]{1,0:T(8,128)(2,1)S(1)}, u32[]{:S(2)}, u32[]{:S(2)}) %collective-permute-start.30) | collective-permute-done | bytes 393248 | tf_op jit(solution)/shard_map/ppermute | solution.py:681
  230.2 7.0 %collective-permute-done.38.refs_6_ = bf16[256,512]{1,0:T(8,128)(2,1)S(1)} collective-permute-done((bf16[256,512]{1,0:T(8,128)(2,1)S(1)}, bf16[256,512]{1,0:T(8,128)(2,1)S(1)}, u32[]{:S(2)}, u32[]{:S(2)}) %collective-permute-start.38) | collective-permute-done | bytes 262176 | tf_op jit(solution)/shard_map/ppermute | solution.py:681
  238.3 8.4 %collective-permute-done.39 = bf16[256,768]{1,0:T(8,128)(2,1)S(1)} collective-permute-done((bf16[256,768]{1,0:T(8,128)(2,1)S(1)}, bf16[256,768]{1,0:T(8,128)(2,1)S(1)}, u32[]{:S(2)}, u32[]{:S(2)}) %collective-permute-start.39) | collective-permute-done | bytes 393248 | tf_op jit(solution)/shard_map/ppermute | solution.py:681
  248.2 16.7 %collective-permute-done.44.refs_7_ = bf16[256,512]{1,0:T(8,128)(2,1)S(1)} collective-permute-done((bf16[256,512]{1,0:T(8,128)(2,1)S(1)}, bf16[256,512]{1,0:T(8,128)(2,1)S(1)}, u32[]{:S(2)}, u32[]{:S(2)}) %collective-permute-start.44) | collective-permute-done | bytes 262176 | tf_op jit(solution)/shard_map/ppermute | solution.py:681
  270.3 9.5 %collective-permute-done.58.refs_15_.refs_7_ = bf16[1024,256]{1,0:T(8,128)(2,1)S(1)} collective-permute-done((bf16[1024,256]{1,0:T(8,128)(2,1)S(1)}, bf16[1024,256]{1,0:T(8,128)(2,1)S(1)}, u32[]{:S(2)}, u32[]{:S(2)}) %collective-permute-start.58) | collective-permute-done | bytes 524320 | tf_op jit(solution)/shard_map/ppermute | solution.py:681
  282.4 8.7 %collective-permute-done.51.refs_15_.refs_3_ = bf16[1024,256]{1,0:T(8,128)(2,1)S(1)} collective-permute-done((bf16[1024,256]{1,0:T(8,128)(2,1)S(1)}, bf16[1024,256]{1,0:T(8,128)(2,1)S(1)}, u32[]{:S(2)}, u32[]{:S(2)}) %collective-permute-start.51) | collective-permute-done | bytes 524320 | tf_op jit(solution)/shard_map/ppermute | solution.py:681
  293.5 8.8 %collective-permute-done.53.refs_12_.refs_6_ = bf16[1024,256]{1,0:T(8,128)(2,1)S(1)} collective-permute-done((bf16[1024,256]{1,0:T(8,128)(2,1)S(1)}, bf16[1024,256]{1,0:T(8,128)(2,1)S(1)}, u32[]{:S(2)}, u32[]{:S(2)}) %collective-permute-start.53) | collective-permute-done | bytes 524320 | tf_op jit(solution)/shard_map/ppermute | solution.py:681
  302.3 10.8 %collective-permute-done.54.refs_13_.refs_7_ = bf16[1024,256]{1,0:T(8,128)(2,1)S(1)} collective-permute-done((bf16[1024,256]{1,0:T(8,128)(2,1)S(1)}, bf16[1024,256]{1,0:T(8,128)(2,1)S(1)}, u32[]{:S(2)}, u32[]{:S(2)}) %collective-permute-start.54) | collective-permute-done | bytes 524320 | tf_op jit(solution)/shard_map/ppermute | solution.py:681
  313.8 3.5 shard_map.190.refs_0_.refs_4_
  321.1 3.2 shard_map.194
  352.8 9.3 %collective-permute-done.70.x_ref = bf16[256,1024]{1,0:T(8,128)(2,1)S(1)} collective-permute-done((bf16[256,1024]{1,0:T(8,128)(2,1)S(1)}, bf16[256,1024]{1,0:T(8,128)(2,1)S(1)}, u32[]{:S(2)}, u32[]{:S(2)}) %collective-permute-start.70) | collective-permute-done | bytes 524320 | tf_op jit(solution)/shard_map/ppermute | solution.py:684
  369.1 9.8 %collective-permute-done.71.x_ref = bf16[256,1024]{1,0:T(8,128)(2,1)S(1)} collective-permute-done((bf16[256,1024]{1,0:T(8,128)(2,1)S(1)}, bf16[256,1024]{1,0:T(8,128)(2,1)S(1)}, u32[]{:S(2)}, u32[]{:S(2)}) %collective-permute-start.71) | collective-permute-done | bytes 524320 | tf_op jit(solution)/shard_map/ppermute | solution.py:684
  385.8 5.7 %shard_map.201 = (f32[128,1280]{1,0:T(8,128)}, bf16[128,128]{1,0:T(8,128)(2,1)}) custom-call(f32[128,2048]{1,0:T(8,128)} %copy-done.33, bf16[128,2048]{1,0:T(8,128)(2,1)} %copy-done.48, bf16[128,2048]{1,0:T(8,128)(2,1)} %collective-permute-done.73.r2, bf16[128,128]{1,0:T(8,128)(2,1)} %copy-done.30, bf16[64,2048]{1,0:T(8,128)(2,1)} %qo.17, ...), custom_call_target="tpu_custom_call" | custom-call | flops 1 | bytes 1 | tf_op jit(solution)/shard_map/pallas_call | solution.py:384
  392.2 3.4 collective-permute-done.75.refs_1_
  405.9 4.6 %collective-permute-done.79 = bf16[16,5376]{1,0:T(8,128)(2,1)S(1)} collective-permute-done((bf16[16,5376]{1,0:T(8,128)(2,1)S(1)}, bf16[16,5376]{1,0:T(8,128)(2,1)S(1)}, u32[]{:S(2)}, u32[]{:S(2)}) %collective-permute-start.79) | collective-permute-done | bytes 172064 | tf_op jit(solution)/shard_map/ppermute | solution.py:681
  415.1 5.5 %collective-permute-done.80 = bf16[8,5376]{1,0:T(8,128)(2,1)S(1)} collective-permute-done((bf16[8,5376]{1,0:T(8,128)(2,1)S(1)}, bf16[8,5376]{1,0:T(8,128)(2,1)S(1)}, u32[]{:S(2)}, u32[]{:S(2)}) %collective-permute-start.80) | collective-permute-done | bytes 86048 | tf_op jit(solution)/shard_map/ppermute | solution.py:681
  420.7 6.5 %collective-permute-done.81 = bf16[8,5376]{1,0:T(8,128)(2,1)S(1)} collective-permute-done((bf16[8,5376]{1,0:T(8,128)(2,1)S(1)}, bf16[8,5376]{1,0:T(8,128)(2,1)S(1)}, u32[]{:S(2)}, u32[]{:S(2)}) %collective-permute-start.81) | collective-permute-done | bytes 86048 | tf_op jit(solution)/shard_map/ppermute | solution.py:681
  427.3 3.1 collective-permute-start.83
  430.8 4.6 %collective-permute-done.82 = bf16[16,5376]{1,0:T(8,128)(2,1)S(1)} collective-permute-done((bf16[16,5376]{1,0:T(8,128)(2,1)S(1)}, bf16[16,5376]{1,0:T(8,128)(2,1)S(1)}, u32[]{:S(2)}, u32[]{:S(2)}) %collective-permute-start.82) | collective-permute-done | bytes 172064 | tf_op jit(solution)/shard_map/ppermute | solution.py:681
  (375 shorter events, 153.2 us)
Async XLA Ops:
  3.6 53.2 %collective-permute-start.5 = (bf16[512,768]{1,0:T(8,128)(2,1)S(1)}, bf16[512,768]{1,0:T(8,128)(2,1)S(1)}, u32[]{:S(2)}, u32[]{:S(2)}) collective-permute-start(bf16[512,768]{1,0:T(8,128)(2,1)S(1)} %pad_maximum_fusion.1.refs_0_), channel_id=1, source_target_pairs={{0,4},{2,6},{4,0},{6,2},{8,12},{10,14},{12,8},{14,10},{16,20},{18,... | collective-permute-start | bytes 2359304 | tf_op jit(solution)/shard_map/ppermute | solution.py:681
  6.7 50.2 %collective-permute-start.6 = (bf16[512,768]{1,0:T(8,128)(2,1)S(1)}, bf16[512,768]{1,0:T(8,128)(2,1)}, u32[]{:S(2)}, u32[]{:S(2)}) collective-permute-start(bf16[512,768]{1,0:T(8,128)(2,1)S(1)} %pad_maximum_fusion.1.refs_0_), channel_id=1, source_target_pairs={{0,16},{2,18},{4,20},{6,22},{8,24},{10,26},{12,28},{14,30},{16,0},... | collective-permute-start | bytes 2359304 | tf_op jit(solution)/shard_map/ppermute | solution.py:681
  16.7 31.0 %collective-permute-start = (bf16[1,128,2048]{2,1,0:T(8,128)(2,1)}, bf16[1,128,2048]{2,1,0:T(8,128)(2,1)}, u32[]{:S(2)}, u32[]{:S(2)}) collective-permute-start(bf16[1,128,2048]{2,1,0:T(8,128)(2,1)} %get-tuple-element.108), channel_id=1, source_target_pairs={{0,8},{2,10},{4,12},{6,14},{8,0},{10,2},{12,4},{14,6},{16,24},{18,... | collective-permute-start | bytes 1572872 | tf_op jit(solution)/shard_map/ppermute | solution.py:681
  18.3 45.2 %collective-permute-start.2 = (bf16[2,128,2048]{2,1,0:T(8,128)(2,1)}, bf16[2,128,2048]{2,1,0:T(8,128)(2,1)}, u32[]{:S(2)}, u32[]{:S(2)}) collective-permute-start(bf16[2,128,2048]{2,1,0:T(8,128)(2,1)} %get-tuple-element.109), channel_id=1, source_target_pairs={{0,2},{2,0},{4,6},{6,4},{8,10},{10,8},{12,14},{14,12},{16,18},{18,... | collective-permute-start | bytes 3145736 | tf_op jit(solution)/shard_map/ppermute | solution.py:681
  18.3 37.0 %collective-permute-start.3 = (bf16[1,128,2048]{2,1,0:T(8,128)(2,1)}, bf16[1,128,2048]{2,1,0:T(8,128)(2,1)}, u32[]{:S(2)}, u32[]{:S(2)}) collective-permute-start(bf16[1,128,2048]{2,1,0:T(8,128)(2,1)} %get-tuple-element.110), channel_id=1, source_target_pairs={{0,10},{2,8},{4,14},{6,12},{8,2},{10,0},{12,6},{14,4},{16,26},{18,... | collective-permute-start | bytes 1572872 | tf_op jit(solution)/shard_map/ppermute | solution.py:681
  56.9 37.8 %collective-permute-start.8 = (bf16[512,768]{1,0:T(8,128)(2,1)S(1)}, bf16[512,768]{1,0:T(8,128)(2,1)S(1)}, u32[]{:S(2)}, u32[]{:S(2)}) collective-permute-start(bf16[512,768]{1,0:T(8,128)(2,1)S(1)} %pad_maximum_fusion.2.refs_0_), channel_id=1, source_target_pairs={{0,16},{2,18},{4,20},{6,22},{8,24},{10,26},{12,28},{14,30},{16,0},... | collective-permute-start | bytes 2359304 | tf_op jit(solution)/shard_map/ppermute | solution.py:681
  59.1 35.6 %collective-permute-start.9 = (bf16[512,768]{1,0:T(8,128)(2,1)S(1)}, bf16[512,768]{1,0:T(8,128)(2,1)S(1)}, u32[]{:S(2)}, u32[]{:S(2)}) collective-permute-start(bf16[512,768]{1,0:T(8,128)(2,1)S(1)} %pad_maximum_fusion.2.refs_0_), channel_id=1, source_target_pairs={{0,4},{2,6},{4,0},{6,2},{8,12},{10,14},{12,8},{14,10},{16,20},{18,... | collective-permute-start | bytes 2359304 | tf_op jit(solution)/shard_map/ppermute | solution.py:681
  59.6 35.4 %collective-permute-start.7 = (bf16[512,768]{1,0:T(8,128)(2,1)}, bf16[512,768]{1,0:T(8,128)(2,1)S(1)}, u32[]{:S(2)}, u32[]{:S(2)}) collective-permute-start(bf16[512,768]{1,0:T(8,128)(2,1)} %collective-permute-done.6.refs_2_), channel_id=1, source_target_pairs={{0,4},{2,6},{4,0},{6,2},{8,12},{10,14},{12,8},{14,10},{16,20},{18,... | collective-permute-start | bytes 2359304 | tf_op jit(solution)/shard_map/ppermute | solution.py:681
  99.7 37.6 %collective-permute-start.15 = (bf16[512,768]{1,0:T(8,128)(2,1)S(1)}, bf16[512,768]{1,0:T(8,128)(2,1)S(1)}, u32[]{:S(2)}, u32[]{:S(2)}) collective-permute-start(bf16[512,768]{1,0:T(8,128)(2,1)S(1)} %pad_maximum_fusion.4.refs_0_), channel_id=1, source_target_pairs={{0,16},{2,18},{4,20},{6,22},{8,24},{10,26},{12,28},{14,30},{16,0},... | collective-permute-start | bytes 2359304 | tf_op jit(solution)/shard_map/ppermute | solution.py:681
  100.6 36.6 %collective-permute-start.16 = (bf16[512,768]{1,0:T(8,128)(2,1)S(1)}, bf16[512,768]{1,0:T(8,128)(2,1)S(1)}, u32[]{:S(2)}, u32[]{:S(2)}) collective-permute-start(bf16[512,768]{1,0:T(8,128)(2,1)S(1)} %pad_maximum_fusion.4.refs_0_), channel_id=1, source_target_pairs={{0,4},{2,6},{4,0},{6,2},{8,12},{10,14},{12,8},{14,10},{16,20},{18,... | collective-permute-start | bytes 2359304 | tf_op jit(solution)/shard_map/ppermute | solution.py:681
  101.2 36.6 %collective-permute-start.14 = (bf16[512,768]{1,0:T(8,128)(2,1)S(1)}, bf16[512,768]{1,0:T(8,128)(2,1)S(1)}, u32[]{:S(2)}, u32[]{:S(2)}) collective-permute-start(bf16[512,768]{1,0:T(8,128)(2,1)S(1)} %collective-permute-done.8.refs_2_), channel_id=1, source_target_pairs={{0,4},{2,6},{4,0},{6,2},{8,12},{10,14},{12,8},{14,10},{16,20},{18,... | collective-permute-start | bytes 2359304 | tf_op jit(solution)/shard_map/ppermute | solution.py:681
  106.5 37.0 %collective-permute-start.13 = (bf16[256,768]{1,0:T(8,128)(2,1)S(1)}, bf16[256,768]{1,0:T(8,128)(2,1)S(1)}, u32[]{:S(2)}, u32[]{:S(2)}) collective-permute-start(bf16[256,768]{1,0:T(8,128)(2,1)S(1)} %pad_maximum_fusion.10), channel_id=1, source_target_pairs={{0,8},{2,10},{4,12},{6,14},{8,0},{10,2},{12,4},{14,6},{16,24},{18,... | collective-permute-start | bytes 1179656 | tf_op jit(solution)/shard_map/ppermute | solution.py:681
  137.2 36.6 %collective-permute-start.23 = (bf16[512,768]{1,0:T(8,128)(2,1)S(1)}, bf16[512,768]{1,0:T(8,128)(2,1)S(1)}, u32[]{:S(2)}, u32[]{:S(2)}) collective-permute-start(bf16[512,768]{1,0:T(8,128)(2,1)S(1)} %pad_maximum_fusion.3.refs_0_), channel_id=1, source_target_pairs={{0,16},{2,18},{4,20},{6,22},{8,24},{10,26},{12,28},{14,30},{16,0},... | collective-permute-start | bytes 2359304 | tf_op jit(solution)/shard_map/ppermute | solution.py:681
  137.2 36.6 %collective-permute-start.24 = (bf16[512,768]{1,0:T(8,128)(2,1)S(1)}, bf16[512,768]{1,0:T(8,128)(2,1)S(1)}, u32[]{:S(2)}, u32[]{:S(2)}) collective-permute-start(bf16[512,768]{1,0:T(8,128)(2,1)S(1)} %pad_maximum_fusion.3.refs_0_), channel_id=1, source_target_pairs={{0,4},{2,6},{4,0},{6,2},{8,12},{10,14},{12,8},{14,10},{16,20},{18,... | collective-permute-start | bytes 2359304 | tf_op jit(solution)/shard_map/ppermute | solution.py:681
  143.5 30.4 %collective-permute-start.22 = (bf16[512,768]{1,0:T(8,128)(2,1)S(1)}, bf16[512,768]{1,0:T(8,128)(2,1)S(1)}, u32[]{:S(2)}, u32[]{:S(2)}) collective-permute-start(bf16[512,768]{1,0:T(8,128)(2,1)S(1)} %collective-permute-done.15.refs_2_), channel_id=1, source_target_pairs={{0,4},{2,6},{4,0},{6,2},{8,12},{10,14},{12,8},{14,10},{16,20},{18,... | collective-permute-start | bytes 2359304 | tf_op jit(solution)/shard_map/ppermute | solution.py:681
  159.8 22.5 %collective-permute-start.21 = (bf16[256,768]{1,0:T(8,128)(2,1)S(1)}, bf16[256,768]{1,0:T(8,128)(2,1)S(1)}, u32[]{:S(2)}, u32[]{:S(2)}) collective-permute-start(bf16[256,768]{1,0:T(8,128)(2,1)S(1)} %pad_maximum_fusion.11), channel_id=1, source_target_pairs={{0,8},{2,10},{4,12},{6,14},{8,0},{10,2},{12,4},{14,6},{16,24},{18,... | collective-permute-start | bytes 1179656 | tf_op jit(solution)/shard_map/ppermute | solution.py:681
  162.3 21.7 %collective-permute-start.28 = (bf16[512,512]{1,0:T(8,128)(2,1)S(1)}, bf16[512,512]{1,0:T(8,128)(2,1)S(1)}, u32[]{:S(2)}, u32[]{:S(2)}) collective-permute-start(bf16[512,512]{1,0:T(8,128)(2,1)S(1)} %pad_maximum_fusion.6), channel_id=1, source_target_pairs={{0,2},{2,0},{4,6},{6,4},{8,10},{10,8},{12,14},{14,12},{16,18},{18,... | collective-permute-start | bytes 1572872 | tf_op jit(solution)/shard_map/ppermute | solution.py:681
  173.9 25.4 %collective-permute-start.32 = (bf16[1024,256]{1,0:T(8,128)(2,1)S(1)}, bf16[1024,256]{1,0:T(8,128)(2,1)S(1)}, u32[]{:S(2)}, u32[]{:S(2)}) collective-permute-start(bf16[1024,256]{1,0:T(8,128)(2,1)S(1)} %constant_dynamic-slice_fusion.1.refs_12_.refs_0_), channel_id=1, source_target_pairs={{0,16},{2,18},{4,20},{6,22},{8,24},{10,26},{12,28},{14,30},{16,0},... | collective-permute-start | bytes 1572872 | tf_op jit(solution)/shard_map/ppermute | solution.py:681
  184.0 29.9 %collective-permute-start.31 = (bf16[512,768]{1,0:T(8,128)(2,1)S(1)}, bf16[512,768]{1,0:T(8,128)(2,1)S(1)}, u32[]{:S(2)}, u32[]{:S(2)}) collective-permute-start(bf16[512,768]{1,0:T(8,128)(2,1)S(1)} %collective-permute-done.23.refs_2_), channel_id=1, source_target_pairs={{0,4},{2,6},{4,0},{6,2},{8,12},{10,14},{12,8},{14,10},{16,20},{18,... | collective-permute-start | bytes 2359304 | tf_op jit(solution)/shard_map/ppermute | solution.py:681
  199.3 37.9 %collective-permute-start.40 = (bf16[1024,256]{1,0:T(8,128)(2,1)S(1)}, bf16[1024,256]{1,0:T(8,128)(2,1)S(1)}, u32[]{:S(2)}, u32[]{:S(2)}) collective-permute-start(bf16[1024,256]{1,0:T(8,128)(2,1)S(1)} %constant_dynamic-slice_fusion.3.refs_13_.refs_1_), channel_id=1, source_target_pairs={{0,16},{2,18},{4,20},{6,22},{8,24},{10,26},{12,28},{14,30},{16,0},... | collective-permute-start | bytes 1572872 | tf_op jit(solution)/shard_map/ppermute | solution.py:681
  199.4 37.9 %collective-permute-start.41 = (bf16[1024,256]{1,0:T(8,128)(2,1)S(1)}, bf16[1024,256]{1,0:T(8,128)(2,1)S(1)}, u32[]{:S(2)}, u32[]{:S(2)}) collective-permute-start(bf16[1024,256]{1,0:T(8,128)(2,1)S(1)} %constant_dynamic-slice_fusion.3.refs_13_.refs_1_), channel_id=1, source_target_pairs={{0,4},{2,6},{4,0},{6,2},{8,12},{10,14},{12,8},{14,10},{16,20},{18,... | collective-permute-start | bytes 1572872 | tf_op jit(solution)/shard_map/ppermute | solution.py:681
  204.5 21.7 %collective-permute-start.30 = (bf16[256,768]{1,0:T(8,128)(2,1)S(1)}, bf16[256,768]{1,0:T(8,128)(2,1)S(1)}, u32[]{:S(2)}, u32[]{:S(2)}) collective-permute-start(bf16[256,768]{1,0:T(8,128)(2,1)S(1)} %pad_maximum_fusion.12), channel_id=1, source_target_pairs={{0,8},{2,10},{4,12},{6,14},{8,0},{10,2},{12,4},{14,6},{16,24},{18,... | collective-permute-start | bytes 1179656 | tf_op jit(solution)/shard_map/ppermute | solution.py:681
  204.6 23.4 %collective-permute-start.37 = (bf16[512,512]{1,0:T(8,128)(2,1)S(1)}, bf16[512,512]{1,0:T(8,128)(2,1)S(1)}, u32[]{:S(2)}, u32[]{:S(2)}) collective-permute-start(bf16[512,512]{1,0:T(8,128)(2,1)S(1)} %pad_maximum_fusion.7), channel_id=1, source_target_pairs={{0,2},{2,0},{4,6},{6,4},{8,10},{10,8},{12,14},{14,12},{16,18},{18,... | collective-permute-start | bytes 1572872 | tf_op jit(solution)/shard_map/ppermute | solution.py:681
  237.8 27.2 %collective-permute-start.49 = (bf16[1024,256]{1,0:T(8,128)(2,1)S(1)}, bf16[1024,256]{1,0:T(8,128)(2,1)S(1)}, u32[]{:S(2)}, u32[]{:S(2)}) collective-permute-start(bf16[1024,256]{1,0:T(8,128)(2,1)S(1)} %get-tuple-element.178.refs_12_.refs_0_), channel_id=1, source_target_pairs={{0,4},{2,6},{4,0},{6,2},{8,12},{10,14},{12,8},{14,10},{16,20},{18,... | collective-permute-start | bytes 1572872 | tf_op jit(solution)/shard_map/ppermute | solution.py:681
  238.3 26.8 %collective-permute-start.50 = (bf16[1024,256]{1,0:T(8,128)(2,1)S(1)}, bf16[1024,256]{1,0:T(8,128)(2,1)S(1)}, u32[]{:S(2)}, u32[]{:S(2)}) collective-permute-start(bf16[1024,256]{1,0:T(8,128)(2,1)S(1)} %get-tuple-element.178.refs_12_.refs_0_), channel_id=1, source_target_pairs={{0,16},{2,18},{4,20},{6,22},{8,24},{10,26},{12,28},{14,30},{16,0},... | collective-permute-start | bytes 1572872 | tf_op jit(solution)/shard_map/ppermute | solution.py:681
  248.1 22.2 %collective-permute-start.57 = (bf16[1024,256]{1,0:T(8,128)(2,1)S(1)}, bf16[1024,256]{1,0:T(8,128)(2,1)S(1)}, u32[]{:S(2)}, u32[]{:S(2)}) collective-permute-start(bf16[1024,256]{1,0:T(8,128)(2,1)S(1)} %collective-permute-done.32.refs_12_.refs_4_), channel_id=1, source_target_pairs={{0,4},{2,6},{4,0},{6,2},{8,12},{10,14},{12,8},{14,10},{16,20},{18,... | collective-permute-start | bytes 1572872 | tf_op jit(solution)/shard_map/ppermute | solution.py:681
  265.6 25.4 %collective-permute-start.51 = (bf16[1024,256]{1,0:T(8,128)(2,1)S(1)}, bf16[1024,256]{1,0:T(8,128)(2,1)S(1)}, u32[]{:S(2)}, u32[]{:S(2)}) collective-permute-start(bf16[1024,256]{1,0:T(8,128)(2,1)S(1)} %get-tuple-element.179.refs_13_.refs_1_), channel_id=1, source_target_pairs={{0,4},{2,6},{4,0},{6,2},{8,12},{10,14},{12,8},{14,10},{16,20},{18,... | collective-permute-start | bytes 1572872 | tf_op jit(solution)/shard_map/ppermute | solution.py:681
  267.3 25.0 %collective-permute-start.52 = (bf16[1024,256]{1,0:T(8,128)(2,1)S(1)}, bf16[1024,256]{1,0:T(8,128)(2,1)S(1)}, u32[]{:S(2)}, u32[]{:S(2)}) collective-permute-start(bf16[1024,256]{1,0:T(8,128)(2,1)S(1)} %get-tuple-element.179.refs_13_.refs_1_), channel_id=1, source_target_pairs={{0,16},{2,18},{4,20},{6,22},{8,24},{10,26},{12,28},{14,30},{16,0},... | collective-permute-start | bytes 1572872 | tf_op jit(solution)/shard_map/ppermute | solution.py:681
  269.7 51.3 %collective-permute-start.56 = (bf16[2,1024,256]{2,1,0:T(8,128)(2,1)S(1)}, bf16[2,1024,256]{2,1,0:T(8,128)(2,1)S(1)}, u32[]{:S(2)}, u32[]{:S(2)}) collective-permute-start(bf16[2,1024,256]{2,1,0:T(8,128)(2,1)S(1)} %shard_map.192), channel_id=1, source_target_pairs={{0,1},{1,0},{2,3},{3,2},{4,5},{5,4},{6,7},{7,6},{8,9},{9,8},{10,11... | collective-permute-start | bytes 3145736 | tf_op jit(solution)/shard_map/ppermute | solution.py:684
  282.1 38.9 %collective-permute-start.59 = (bf16[2,1024,256]{2,1,0:T(8,128)(2,1)S(1)}, bf16[2,1024,256]{2,1,0:T(8,128)(2,1)S(1)}, u32[]{:S(2)}, u32[]{:S(2)}) collective-permute-start(bf16[2,1024,256]{2,1,0:T(8,128)(2,1)S(1)} %shard_map.193), channel_id=1, source_target_pairs={{0,1},{1,0},{2,3},{3,2},{4,5},{5,4},{6,7},{7,6},{8,9},{9,8},{10,11... | collective-permute-start | bytes 3145736 | tf_op jit(solution)/shard_map/ppermute | solution.py:684
  292.4 20.7 %collective-permute-start.54 = (bf16[1024,256]{1,0:T(8,128)(2,1)S(1)}, bf16[1024,256]{1,0:T(8,128)(2,1)S(1)}, u32[]{:S(2)}, u32[]{:S(2)}) collective-permute-start(bf16[1024,256]{1,0:T(8,128)(2,1)S(1)} %collective-permute-done.52.refs_17_.refs_5_), channel_id=1, source_target_pairs={{0,4},{2,6},{4,0},{6,2},{8,12},{10,14},{12,8},{14,10},{16,20},{18,... | collective-permute-start | bytes 1572872 | tf_op jit(solution)/shard_map/ppermute | solution.py:681
  293.5 25.1 %collective-permute-start.48 = (bf16[128,1024]{1,0:T(8,128)(2,1)S(1)}, bf16[128,1024]{1,0:T(8,128)(2,1)S(1)}, u32[]{:S(2)}, u32[]{:S(2)}) collective-permute-start(bf16[128,1024]{1,0:T(8,128)(2,1)S(1)} %copy-done.60), channel_id=1, source_target_pairs={{0,10},{2,8},{4,14},{6,12},{8,2},{10,0},{12,6},{14,4},{16,26},{18,... | collective-permute-start | bytes 786440 | tf_op jit(solution)/shard_map/ppermute | solution.py:681
  (124 other events, 1874.8 us)
